TPU v7x, 32 devices: a whole 2x2x4 slice. The times are simulated.
32 devices in a mesh: groups: 1, expert: 32 (over z, y, x, core).
Axes of the slice: x: 2, y: 2, z: 4, core: 2. Of those that a mesh axis runs over, the one named last changes fastest.
Arguments:
- tokens: bfloat16 [4096, 2048], P(('groups', 'expert')), may hold values from -6 to 6
- cotangent: bfloat16 [4096, 2048], P(('groups', 'expert')), may hold values from -6 to 6
- token_experts: int32 [4096, 6], P(('groups', 'expert')), may hold values from 0 to 15, all different within a row; in each aligned block of 128 rows (0 to 127, 128 to 255, ...) at most 56 rows name the same one
- routing_weight_cache: float32 [4096, 6], P(('groups', 'expert')), may hold values from 0.05 to 0.5
- gate_weight: bfloat16 [32, 2048, 352], P('expert'), may hold values from -0.125 to 0.125
- up_weight: bfloat16 [32, 2048, 352], P('expert'), may hold values from -0.125 to 0.125
- down_weight: bfloat16 [32, 352, 2048], P('expert'), may hold values from -0.21875 to 0.21875
- gate_adapter_input: bfloat16 [32, 1024, 64], P('expert'), may hold values from -0.125 to 0.125
- gate_adapter_output: bfloat16 [32, 64, 352], P('expert'), may hold values from -0.75 to 0.75
- up_adapter_input: bfloat16 [32, 1024, 64], P('expert'), may hold values from -0.125 to 0.125
- up_adapter_output: bfloat16 [32, 64, 352], P('expert'), may hold values from -0.75 to 0.75
Outputs:
- grad_tokens: bfloat16 [4096, 2048], P(('groups', 'expert'))
- grad_a_gate: float32 [32, 1024, 64], P(('groups', 'expert'))
- grad_b_gate: float32 [32, 64, 352], P(('groups', 'expert'))
- grad_a_up: float32 [32, 1024, 64], P(('groups', 'expert'))
- grad_b_up: float32 [32, 64, 352], P(('groups', 'expert'))
Inputs may be any that keep to these rules, and one draw needn't show every extreme that they name: `token_experts`: each row names 6 different experts; within the 128 rows of one device no expert is named more than 56 times.
All inputs are finite; a program needn't handle non-finite values.
Results may differ from a plain program's by a relative error of at most 0.0066.
Values may be sent and summed in bfloat16 or wider, within the bound.
A program may use at most 128 MiB of HBM per device.

v0:
```python
import jax
import jax.numpy as jnp
from jax import lax
from jax.sharding import PartitionSpec as P


def swapped(value, axis, distance):
    mask = 2**distance
    pairs = [(source, source ^ mask) for source in range(lax.axis_size(axis))]
    return lax.ppermute(value, axis, pairs)


def slot_places(token_experts, expert_count, slot_cap):
    flat_ids = token_experts.reshape(-1)
    picks = (flat_ids[:, None] == jnp.arange(expert_count, dtype=jnp.int32)[None, :]).astype(
        jnp.int32
    )
    earlier = jnp.cumsum(picks, axis=0) - picks
    slots = jnp.sum(earlier * picks, axis=1)
    return (flat_ids * slot_cap + slots).reshape(token_experts.shape)


def trans_right(left, right):
    return lax.dot_general(
        left, right, (((1,), (1,)), ((), ())), preferred_element_type=jnp.float32
    )


def trans_left(left, right):
    return lax.dot_general(
        left, right, (((0,), (0,)), ((), ())), preferred_element_type=jnp.float32
    )


def expert_rows(rows_x, rows_dy, params, my_half):
    gate_w, up_w, down_w, a_gate, b_gate, a_up, b_up = params
    rank = a_gate.shape[1]
    half_width = a_gate.shape[0]
    stacked = jnp.concatenate([a_gate, a_up], axis=1)
    partner = swapped(stacked, "expert", 0)
    adapters = jnp.where(
        my_half == 0,
        jnp.concatenate([stacked, partner], axis=0),
        jnp.concatenate([partner, stacked], axis=0),
    )
    zero_rows = jnp.zeros_like(stacked)
    own_only = jnp.where(
        my_half == 0,
        jnp.concatenate([stacked, zero_rows], axis=0),
        jnp.concatenate([zero_rows, stacked], axis=0),
    )
    low_rank = jnp.dot(rows_x, adapters, preferred_element_type=jnp.float32).astype(jnp.bfloat16)
    low_gate = low_rank[:, :rank]
    low_up = low_rank[:, rank:]
    gate = jnp.dot(rows_x, gate_w, preferred_element_type=jnp.float32) + jnp.dot(
        low_gate, b_gate, preferred_element_type=jnp.float32
    )
    upward = jnp.dot(rows_x, up_w, preferred_element_type=jnp.float32) + jnp.dot(
        low_up, b_up, preferred_element_type=jnp.float32
    )
    hidden_grad = trans_right(rows_dy, down_w)
    sigmoid_gate = jax.nn.sigmoid(gate)
    grad_gate = (hidden_grad * upward * sigmoid_gate * (1.0 + gate * (1.0 - sigmoid_gate))).astype(
        jnp.bfloat16
    )
    grad_up = (hidden_grad * gate * sigmoid_gate).astype(jnp.bfloat16)
    back_part = jnp.concatenate(
        [trans_right(grad_gate, b_gate), trans_right(grad_up, b_up)], axis=1
    )
    back = (back_part + swapped(back_part, "expert", 0)).astype(jnp.bfloat16)
    joined_left = jnp.concatenate([grad_gate, grad_up, back], axis=1)
    joined_right = jnp.concatenate([gate_w, up_w, own_only], axis=1)
    row_grads = trans_right(joined_left, joined_right)
    start = my_half * half_width
    columns = lax.dynamic_slice_in_dim(rows_x, start, half_width, 1)
    grad_adapter = trans_left(columns, back)
    grad_bg = trans_left(low_gate, grad_gate)
    grad_bu = trans_left(low_up, grad_up)
    return (row_grads, (grad_adapter[:, :rank], grad_bg, grad_adapter[:, rank:], grad_bu))


def on_device(
    tokens,
    cotangent,
    token_experts,
    routing_weight_cache,
    gate_weight,
    up_weight,
    down_weight,
    gate_adapter_input,
    gate_adapter_output,
    up_adapter_input,
    up_adapter_output,
):
    n_devices = lax.axis_size("expert")
    n_experts = n_devices // 2
    tok_count, width = tokens.shape
    top_count = token_experts.shape[1]
    slot_cap = 2 * max(2, 9 * tok_count * top_count // (16 * n_experts) + 1)
    slot_total = n_experts * slot_cap
    my_half = lax.axis_index("expert") % 2
    places = slot_places(token_experts, n_experts, slot_cap)
    picker = places[None, :, :] == jnp.arange(slot_total, dtype=jnp.int32)[:, None, None]
    pick_mask = jnp.any(picker, axis=2)
    token_pick = pick_mask.astype(jnp.bfloat16)
    slot_weight = jnp.sum(jnp.where(picker, routing_weight_cache[None, :, :], 0.0), axis=(1, 2))
    send_x = jnp.dot(token_pick, tokens, preferred_element_type=jnp.float32).astype(jnp.bfloat16)
    send_dy = (
        jnp.dot(token_pick, cotangent, preferred_element_type=jnp.float32) * slot_weight[:, None]
    ).astype(jnp.bfloat16)
    params = (
        gate_weight[0],
        up_weight[0],
        down_weight[0],
        gate_adapter_input[0],
        gate_adapter_output[0],
        up_adapter_input[0],
        up_adapter_output[0],
    )
    both_x = jnp.broadcast_to(
        send_x.reshape(n_experts, 1, slot_cap, width), (n_experts, 2, slot_cap, width)
    ).reshape(n_devices, slot_cap, width)
    both_dy = jnp.broadcast_to(
        send_dy.reshape(n_experts, 1, slot_cap, width), (n_experts, 2, slot_cap, width)
    ).reshape(n_devices, slot_cap, width)
    recv_x, recv_dy = (
        lax.all_to_all(both_x, "expert", split_axis=0, concat_axis=0, tiled=True),
        lax.all_to_all(both_dy, "expert", split_axis=0, concat_axis=0, tiled=True),
    )
    partial_value, grads = expert_rows(
        recv_x.reshape(-1, width), recv_dy.reshape(-1, width), params, my_half
    )
    returned = lax.all_to_all(
        partial_value.reshape(n_devices, slot_cap, width),
        "expert",
        split_axis=0,
        concat_axis=0,
        tiled=True,
    )
    summed = jnp.sum(returned.reshape(n_experts, 2, slot_cap, width), axis=1).reshape(
        slot_total, width
    )
    pick_exact = pick_mask.astype(jnp.float32)
    grad_tokens = lax.dot_general(
        pick_exact,
        summed,
        (((0,), (0,)), ((), ())),
        precision=lax.Precision.HIGHEST,
        preferred_element_type=jnp.float32,
    ).astype(jnp.bfloat16)
    grad_ag, grad_bg, grad_au, grad_bu = grads
    return (grad_tokens, grad_ag[None], grad_bg[None], grad_au[None], grad_bu[None])


def solution(mesh):
    in_specs = (
        P(("groups", "expert"), None),
        P(("groups", "expert"), None),
        P(("groups", "expert"), None),
        P(("groups", "expert"), None),
        P("expert", None, None),
        P("expert", None, None),
        P("expert", None, None),
        P("expert", None, None),
        P("expert", None, None),
        P("expert", None, None),
        P("expert", None, None),
    )
    out_specs = (
        P(("groups", "expert"), None),
        P(("groups", "expert"), None, None),
        P(("groups", "expert"), None, None),
        P(("groups", "expert"), None, None),
        P(("groups", "expert"), None, None),
    )
    return jax.shard_map(
        on_device, mesh=mesh, in_specs=in_specs, out_specs=out_specs, check_vma=False
    )
```

profile of v0, /device:TPU:24, one launch (start us, length us, event | category | flops | bytes accessed | tf_op | source)
XLA Modules:
  0.0 714.6 jit_solution(13201661988940062255)
XLA Ops:
  0.6 0.0 copy-start
  0.6 0.9 copy.30
  1.6 0.1 eq.48
  1.7 0.1 eq.44
  1.8 1.7 reduce-window.6
  3.6 0.3 slice_reduce_fusion
  3.8 0.1 fusion.36
  3.9 0.1 reduce_sum.30
  4.1 0.1 copy.33
  4.1 0.7 multiply_add_fusion
  4.9 0.4 fusion.16
  5.3 2.1 convolution_convert_fusion
  7.5 4.1 broadcast_in_dim.48
  11.5 5.9 all-to-all-start.1
  17.5 0.4 select_reduce_fusion
  17.8 3.0 multiply_convert_fusion
  20.9 156.0 %all-to-all-done.1 = bf16[32,56,2048]{2,1,0:T(8,128)(2,1)} async-done(((bf16[32,56,2048]{2,1,0:T(8,128)(2,1)}), bf16[32,56,2048]{2,1,0:T(8,128)(2,1)}, u32[]{:S(2)}, u32[]{:S(2)}) %all-to-all-start.1) | async-done | bytes 7340064 | tf_op jit(solution)/shard_map/all_to_all | solution.py:127
  176.9 6.1 broadcast_in_dim.46
  183.0 7.4 %all-to-all-start = ((bf16[32,56,2048]{2,1,0:T(8,128)(2,1)}), bf16[32,56,2048]{2,1,0:T(8,128)(2,1)}, u32[]{:S(2)}, u32[]{:S(2)}) async-start(bf16[32,56,2048]{2,1,0:T(8,128)(2,1)} %bitcast.76), calls=%async_computation | async-start | bytes 14680064 | tf_op jit(solution)/shard_map/all_to_all | solution.py:128
  190.5 0.2 collective-permute-start
  190.7 1.4 collective-permute-done
  192.1 5.7 convolution_convert_fusion.2
  197.9 0.0 copy-start.3
  197.9 0.0 copy-start.5
  197.9 6.2 fusion.47
  204.1 2.0 convolution_add_fusion
  206.1 7.5 %fusion.49 = f32[1792,352]{0,1:T(8,128)} fusion(bf16[1792,2048]{1,0:T(8,128)(2,1)} %bitcast.7, bf16[1,2048,352]{1,2,0:T(8,128)(2,1)S(1)} %copy-done.11), kind=kOutput, calls=%fused_computation.75 | convolution fusion | flops 2583691264 | bytes 11304960 | tf_op jit(solution)/shard_map/dot_general | solution.py:58
  213.5 136.4 %all-to-all-done = bf16[32,56,2048]{2,1,0:T(8,128)(2,1)} async-done(((bf16[32,56,2048]{2,1,0:T(8,128)(2,1)}), bf16[32,56,2048]{2,1,0:T(8,128)(2,1)}, u32[]{:S(2)}, u32[]{:S(2)}) %all-to-all-start) | async-done | bytes 7340064 | tf_op jit(solution)/shard_map/all_to_all | solution.py:128
  350.0 6.9 multiply_convert_fusion.1
  356.8 0.3 fusion.40
  357.2 0.0 copy-start.6
  357.2 1.1 fusion.17
  358.4 0.3 fusion.37
  358.7 0.0 copy-start.14
  358.7 0.1 pad_maximum_fusion
  358.8 0.1 collective-permute-start.1
  358.9 0.1 pad_select_fusion
  359.0 2.3 collective-permute-done.1
  361.3 0.1 add_convert_fusion
  361.5 11.2 %fusion.2 = f32[1792,2048]{1,0:T(8,128)} fusion(bf16[2048,128]{0,1:T(8,128)(2,1)S(1)} %pad_select_fusion, bf16[2048,352]{0,1:T(8,128)(2,1)S(1)} %bitcast.87, bf16[2048,352]{0,1:T(8,128)(2,1)S(1)} %bitcast.88, bf16[1792,128]{0,1:T(8,128)(2,1)S(1)} %add_convert_fusion, bf16[1792,352]{0,1:T(8,128)(2,1)S(1)} %get-tuple-element.7, bf16[1792,352]{0,1:T(8,128)(2,1)S(1)} %fusion.17), kind=kOutput, calls=%fused_computation.5 | convolution fusion | flops 6126075904 | bytes 21069824 | tf_op jit(solution)/shard_map/dot_general | solution.py:24
  372.7 7.6 %all-to-all-start.2 = ((f32[32,56,2048]{2,1,0:T(8,128)}), f32[32,56,2048]{2,1,0:T(8,128)}, u32[]{:S(2)}, u32[]{:S(2)}) async-start(f32[32,56,2048]{2,1,0:T(8,128)} %bitcast.80), calls=%async_computation.2 | async-start | bytes 29360128 | tf_op jit(solution)/shard_map/all_to_all | solution.py:133
  380.3 2.1 convolution_bitcast_fusion
  382.3 2.1 convolution_bitcast_fusion.1
  384.4 2.7 fusion
  387.1 0.8 slice_bitcast_fusion
  388.0 309.3 %all-to-all-done.2 = f32[32,56,2048]{2,1,0:T(8,128)} async-done(((f32[32,56,2048]{2,1,0:T(8,128)}), f32[32,56,2048]{2,1,0:T(8,128)}, u32[]{:S(2)}, u32[]{:S(2)}) %all-to-all-start.2) | async-done | bytes 14680096 | tf_op jit(solution)/shard_map/all_to_all | solution.py:133
  697.3 10.5 %bitcast_reduce_fusion = f32[16,56,2048]{2,1,0:T(8,128)} fusion(f32[32,56,2048]{2,1,0:T(8,128)} %all-to-all-done.2), kind=kLoop, calls=%fused_computation | loop fusion | flops 1835008 | bytes 22020096 | tf_op jit(solution)/shard_map/reduce_sum | solution.py:140
  707.7 6.8 convolution_convert_fusion.1
  (30 shorter events, 0.1 us)
Async XLA Ops:
  0.6 349.3 %copy-start = (bf16[1,352,2048]{2,1,0:T(8,128)(2,1)S(1)}, bf16[1,352,2048]{2,1,0:T(8,128)(2,1)}, u32[]{:S(2)}) copy-start(bf16[1,352,2048]{2,1,0:T(8,128)(2,1)} %param.17) | copy-start | bytes 4325380
  11.5 5.9 copy-start.10
  11.5 6.3 copy-start.4
  11.5 165.4 %all-to-all-start.1 = ((bf16[32,56,2048]{2,1,0:T(8,128)(2,1)}), bf16[32,56,2048]{2,1,0:T(8,128)(2,1)}, u32[]{:S(2)}, u32[]{:S(2)}) async-start(bf16[32,56,2048]{2,1,0:T(8,128)(2,1)} %bitcast.77), calls=%async_computation.1 | async-start | bytes 14680064 | tf_op jit(solution)/shard_map/all_to_all | solution.py:127
  183.0 7.4 %copy-start.7 = (bf16[1,1024,64]{1,2,0:T(8,128)(2,1)S(1)}, bf16[1,1024,64]{1,2,0:T(8,128)(2,1)}, u32[]{:S(2)}) copy-start(bf16[1,1024,64]{1,2,0:T(8,128)(2,1)} %param.20) | copy-start | bytes 393220
  183.0 7.5 %copy-start.8 = (bf16[1,1024,64]{1,2,0:T(8,128)(2,1)S(1)}, bf16[1,1024,64]{1,2,0:T(8,128)(2,1)}, u32[]{:S(2)}) copy-start(bf16[1,1024,64]{1,2,0:T(8,128)(2,1)} %param.18) | copy-start | bytes 393220
  183.0 166.9 %all-to-all-start = ((bf16[32,56,2048]{2,1,0:T(8,128)(2,1)}), bf16[32,56,2048]{2,1,0:T(8,128)(2,1)}, u32[]{:S(2)}, u32[]{:S(2)}) async-start(bf16[32,56,2048]{2,1,0:T(8,128)(2,1)} %bitcast.76), calls=%async_computation | async-start | bytes 14680064 | tf_op jit(solution)/shard_map/all_to_all | solution.py:128
  190.5 1.6 collective-permute-start
  192.1 5.7 copy-start.13
  197.9 159.3 %copy-start.3 = (bf16[1792,128]{0,1:T(8,128)(2,1)}, bf16[1792,128]{0,1:T(8,128)(2,1)S(1)}, u32[]{:S(2)}) copy-start(bf16[1792,128]{0,1:T(8,128)(2,1)S(1)} %convolution_convert_fusion.2) | copy-start | bytes 1376260
  197.9 6.2 copy-start.5
  204.1 2.0 copy-start.11
  349.9 6.9 copy-start.9
  350.0 7.2 %copy-start.2 = (f32[1792,352]{0,1:T(8,128)S(1)}, f32[1792,352]{0,1:T(8,128)}, u32[]{:S(2)}) copy-start(f32[1792,352]{0,1:T(8,128)} %convolution_add_fusion) | copy-start | bytes 7569412
  350.0 7.2 %copy-start.15 = (f32[1792,352]{0,1:T(8,128)S(1)}, f32[1792,352]{0,1:T(8,128)}, u32[]{:S(2)}) copy-start(f32[1792,352]{0,1:T(8,128)} %fusion.49) | copy-start | bytes 7569412
  357.2 1.2 copy-start.6
  358.7 2.7 copy-start.12
  358.7 2.7 copy-start.14
  358.8 2.5 collective-permute-start.1
  372.7 324.6 %all-to-all-start.2 = ((f32[32,56,2048]{2,1,0:T(8,128)}), f32[32,56,2048]{2,1,0:T(8,128)}, u32[]{:S(2)}, u32[]{:S(2)}) async-start(f32[32,56,2048]{2,1,0:T(8,128)} %bitcast.80), calls=%async_computation.2 | async-start | bytes 29360128 | tf_op jit(solution)/shard_map/all_to_all | solution.py:133
  707.7 6.8 copy-start.1
where the time goes:
time: 726 us; the launch traced here: 715 us
  waiting for transfers between devices  605 us (83%)
  matrix products  60 us (8%)
  starting transfers between devices  21.3 us (3%)
  other arithmetic  14.1 us (2%)
  local copies, waits for them, and re-layouts  12.7 us (2%)
    all_to_all x1, waiting for transfers between devices, on_device(): lax.all_to_all(partial_value.reshape(n_devices, slot_cap, width), 'expert...  309 us
    all_to_all x1, waiting for transfers between devices, on_device(): lax.all_to_all(both_x, 'expert', split_axis=0, concat_axis=0, tiled=True)  156 us
    all_to_all x1, waiting for transfers between devices, on_device(): lax.all_to_all(both_dy, 'expert', split_axis=0, concat_axis=0, tiled=True)  136 us
    dot_general x4, matrix products, trans_right(): lax.dot_general(left, right, (((1,), (1,)), ((), ())), preferred_element_...  18.7 us
  transfers between devices with their start and end apart: 5, of which 5 were waited for; matrix products, arithmetic and copies ran while one was open for 5% of the time, Pallas kernels for 0%

commit v1 on v0

v1 whole, which is shorter than its diff:
```python
import jax
import jax.numpy as jnp
from jax import lax
from jax.sharding import PartitionSpec as P


def swapped(value, axis, distance):
    mask = 2**distance
    pairs = [(source, source ^ mask) for source in range(lax.axis_size(axis))]
    return lax.ppermute(value, axis, pairs)


def slot_places(token_experts, expert_count, slot_cap):
    flat_ids = token_experts.reshape(-1)
    picks = (flat_ids[:, None] == jnp.arange(expert_count, dtype=jnp.int32)[None, :]).astype(
        jnp.int32
    )
    earlier = jnp.cumsum(picks, axis=0) - picks
    slots = jnp.sum(earlier * picks, axis=1)
    return (flat_ids * slot_cap + slots).reshape(token_experts.shape)


def trans_right(left, right):
    return lax.dot_general(
        left, right, (((1,), (1,)), ((), ())), preferred_element_type=jnp.float32
    )


def trans_left(left, right):
    return lax.dot_general(
        left, right, (((0,), (0,)), ((), ())), preferred_element_type=jnp.float32
    )


def joined(own, axis, my_half):
    other = swapped(own, "expert", 0)
    first = jnp.where(my_half == 0, own, other)
    second = jnp.where(my_half == 0, other, own)
    return jnp.concatenate([first, second], axis=axis)


def half_sum(whole, axis, my_half):
    size = whole.shape[axis] // 2
    kept = lax.dynamic_slice_in_dim(whole, my_half * size, size, axis)
    given = lax.dynamic_slice_in_dim(whole, (1 - my_half) * size, size, axis)
    return kept + swapped(given, "expert", 0)


def expert_rows(rows_x, rows_dy, params, my_half):
    gate_w, up_w, down_w, adapters, b_gate, b_up = params
    rank = b_gate.shape[0]
    low_rank = jnp.dot(rows_x, adapters, preferred_element_type=jnp.float32).astype(jnp.bfloat16)
    low_gate = low_rank[:, :rank]
    low_up = low_rank[:, rank:]
    gate = jnp.dot(rows_x, gate_w, preferred_element_type=jnp.float32) + jnp.dot(
        low_gate, b_gate, preferred_element_type=jnp.float32
    )
    upward = jnp.dot(rows_x, up_w, preferred_element_type=jnp.float32) + jnp.dot(
        low_up, b_up, preferred_element_type=jnp.float32
    )
    hidden_grad = trans_right(rows_dy, down_w)
    sigmoid_gate = jax.nn.sigmoid(gate)
    grad_gate = (hidden_grad * upward * sigmoid_gate * (1.0 + gate * (1.0 - sigmoid_gate))).astype(
        jnp.bfloat16
    )
    grad_up = (hidden_grad * gate * sigmoid_gate).astype(jnp.bfloat16)
    back = jnp.concatenate(
        [trans_right(grad_gate, b_gate), trans_right(grad_up, b_up)], axis=1
    ).astype(jnp.bfloat16)
    row_grads = (
        trans_right(grad_gate, gate_w) + trans_right(grad_up, up_w) + trans_right(back, adapters)
    ).astype(jnp.bfloat16)
    grad_adapter = half_sum(trans_left(rows_x, back), 0, my_half)
    grad_b = jnp.stack([trans_left(low_gate, grad_gate), trans_left(low_up, grad_up)])
    grad_b = half_sum(grad_b, 2, my_half)
    return (row_grads, (grad_adapter[:, :rank], grad_b[0], grad_adapter[:, rank:], grad_b[1]))


def on_device(
    tokens,
    cotangent,
    token_experts,
    routing_weight_cache,
    gate_weight,
    up_weight,
    down_weight,
    gate_adapter_input,
    gate_adapter_output,
    up_adapter_input,
    up_adapter_output,
):
    n_devices = lax.axis_size("expert")
    n_experts = n_devices // 2
    tok_count, width = tokens.shape
    top_count = token_experts.shape[1]
    slot_cap = 2 * max(2, 9 * tok_count * top_count // (16 * n_experts) + 1)
    slot_total = n_experts * slot_cap
    my_half = lax.axis_index("expert") % 2
    same_half = [list(range(half, n_devices, 2)) for half in range(2)]
    places = slot_places(token_experts, n_experts, slot_cap)
    picker = places[None, :, :] == jnp.arange(slot_total, dtype=jnp.int32)[:, None, None]
    pick_mask = jnp.any(picker, axis=2)
    token_pick = pick_mask.astype(jnp.bfloat16)
    slot_weight = jnp.sum(jnp.where(picker, routing_weight_cache[None, :, :], 0.0), axis=(1, 2))
    send_x = jnp.dot(token_pick, tokens, preferred_element_type=jnp.float32).astype(jnp.bfloat16)
    send_dy = (
        jnp.dot(token_pick, cotangent, preferred_element_type=jnp.float32) * slot_weight[:, None]
    ).astype(jnp.bfloat16)
    params = (
        joined(gate_weight[0], 1, my_half),
        joined(up_weight[0], 1, my_half),
        joined(down_weight[0], 0, my_half),
        joined(jnp.concatenate([gate_adapter_input[0], up_adapter_input[0]], axis=1), 0, my_half),
        joined(gate_adapter_output[0], 1, my_half),
        joined(up_adapter_output[0], 1, my_half),
    )

    def exchanged(rows):
        return lax.all_to_all(
            rows.reshape(n_experts, slot_cap, width),
            "expert",
            split_axis=0,
            concat_axis=0,
            tiled=True,
            axis_index_groups=same_half,
        ).reshape(slot_total, width)

    row_grads, grads = expert_rows(exchanged(send_x), exchanged(send_dy), params, my_half)
    returned = exchanged(row_grads)
    grad_tokens = trans_left(token_pick, returned).astype(jnp.bfloat16)
    grad_ag, grad_bg, grad_au, grad_bu = grads
    return (grad_tokens, grad_ag[None], grad_bg[None], grad_au[None], grad_bu[None])


def solution(mesh):
    in_specs = (
        P(("groups", "expert"), None),
        P(("groups", "expert"), None),
        P(("groups", "expert"), None),
        P(("groups", "expert"), None),
        P("expert", None, None),
        P("expert", None, None),
        P("expert", None, None),
        P("expert", None, None),
        P("expert", None, None),
        P("expert", None, None),
        P("expert", None, None),
    )
    out_specs = (
        P(("groups", "expert"), None),
        P(("groups", "expert"), None, None),
        P(("groups", "expert"), None, None),
        P(("groups", "expert"), None, None),
        P(("groups", "expert"), None, None),
    )
    return jax.shard_map(
        on_device, mesh=mesh, in_specs=in_specs, out_specs=out_specs, check_vma=False
    )
```

time: 726 us -> 299 us (0.41)
  waiting for transfers between devices: 605 us -> 200 us
  local copies, waits for them, and re-layouts: 12.7 us -> 3.3 us
  matrix products: 60 us -> 51.4 us
    all_to_all x3, waiting for transfers between devices: 602 us -> 195 us  [exchanged(): lax.all_to_all(rows.reshape(n_experts, slot_cap, width), 'expert', split_...]
    reduce_sum x1 -> x0, other arithmetic: 10.5 us -> none  [on_device(): jnp.sum(returned.reshape(n_experts, 2, slot_cap, width), axis=1)]
    broadcast_in_dim x2 -> x0, local copies, waits for them, and re-layouts: 10.2 us -> none  [the longest x1 6.12 us: on_device(): jnp.broadcast_to(send_dy.reshape(n_experts, 1, slot_cap, width), (n_exper...]
    dot_general x4 -> x6, matrix products: 18.7 us -> 17.1 us  [trans_right(): lax.dot_general(left, right, (((1,), (1,)), ((), ())), preferred_element_...]
  transfers between devices with their start and end apart: 5 -> 11, of which waited for: 5 -> 6; matrix products, arithmetic and copies ran while one was open for 5% -> 10% of each run, Pallas kernels for 0% -> 0%
where the time goes in v1:
time: 299 us; the launch traced here: 294 us
  waiting for transfers between devices  200 us (67%)
  matrix products  51.4 us (17%)
  starting transfers between devices  28 us (9%)
  other arithmetic  11 us (4%)
  local copies, waits for them, and re-layouts  3.3 us (1%)
    all_to_all x3, waiting for transfers between devices, exchanged(): lax.all_to_all(rows.reshape(n_experts, slot_cap, width), 'expert', split_...  195 us
    all_to_all x3, starting transfers between devices, exchanged(): lax.all_to_all(rows.reshape(n_experts, slot_cap, width), 'expert', split_...  26 us
    dot_general x6, matrix products, trans_right(): lax.dot_general(left, right, (((1,), (1,)), ((), ())), preferred_element_...  17.1 us
    dot_general x4, matrix products, trans_left(): lax.dot_general(left, right, (((0,), (0,)), ((), ())), preferred_element_...  8.25 us
    select_n x6, other arithmetic, joined(): first = jnp.where(my_half == 0, own, other)  7.35 us
    dot_general x1, matrix products, expert_rows(): jnp.dot(rows_x, gate_w, preferred_element_type=jnp.float32)  6.84 us
    dot_general x1, matrix products, expert_rows(): jnp.dot(rows_x, up_w, preferred_element_type=jnp.float32)  6.67 us
  transfers between devices with their start and end apart: 11, of which 6 were waited for; matrix products, arithmetic and copies ran while one was open for 10% of the time, Pallas kernels for 0%

profile of v1, /device:TPU:24, one launch (start us, length us, event | category | flops | bytes accessed | tf_op | source)
XLA Modules:
  0.0 294.4 jit_solution(15673286731408608360)
XLA Ops:
  0.6 0.9 copy.30
  1.5 0.1 eq.58
  1.6 0.1 eq.54
  1.8 1.7 reduce-window.6
  3.5 0.3 slice_reduce_fusion
  3.8 0.1 fusion.23
  3.9 0.1 reduce_sum.21
  4.1 0.7 multiply_add_fusion
  4.8 0.4 fusion.4
  5.3 3.0 %convolution_convert_fusion = bf16[896,2048]{1,0:T(8,128)(2,1)} fusion(pred[896,128]{1,0:T(8,128)(4,1)S(1)} %fusion.4, bf16[128,2048]{1,0:T(8,128)(2,1)S(1)} %copy-done), kind=kOutput, calls=%fused_computation.2 | convolution fusion | flops 471597056 | bytes 4308992 | tf_op jit(solution)/shard_map/dot_general | solution.py:105
  8.3 7.1 %all-to-all-start.1 = ((bf16[16,56,2048]{2,1,0:T(8,128)(2,1)}), bf16[16,56,2048]{2,1,0:T(8,128)(2,1)}, u32[]{:S(2)}, u32[]{:S(2)}) async-start(bf16[16,56,2048]{2,1,0:T(8,128)(2,1)} %bitcast.68), calls=%async_computation.1 | async-start | bytes 7340032 | tf_op jit(solution)/shard_map/all_to_all | solution.py:119
  15.4 0.4 select_reduce_fusion
  15.8 2.9 multiply_convert_fusion
  18.7 74.9 %all-to-all-done.1 = bf16[16,56,2048]{2,1,0:T(8,128)(2,1)} async-done(((bf16[16,56,2048]{2,1,0:T(8,128)(2,1)}), bf16[16,56,2048]{2,1,0:T(8,128)(2,1)}, u32[]{:S(2)}, u32[]{:S(2)}) %all-to-all-start.1) | async-done | bytes 3670048 | tf_op jit(solution)/shard_map/all_to_all | solution.py:119
  93.7 9.7 %all-to-all-start = ((bf16[16,56,2048]{2,1,0:T(8,128)(2,1)}), bf16[16,56,2048]{2,1,0:T(8,128)(2,1)}, u32[]{:S(2)}, u32[]{:S(2)}) async-start(bf16[16,56,2048]{2,1,0:T(8,128)(2,1)} %bitcast.70), calls=%async_computation | async-start | bytes 7340032 | tf_op jit(solution)/shard_map/all_to_all | solution.py:119
  103.4 0.5 collective-permute-start
  104.0 0.5 collective-permute-start.2
  104.6 3.4 %collective-permute-done.5 = bf16[64,352]{1,0:T(8,128)(2,1)S(1)} collective-permute-done((bf16[64,352]{1,0:T(8,128)(2,1)S(1)}, bf16[64,352]{1,0:T(8,128)(2,1)S(1)}, u32[]{:S(2)}, u32[]{:S(2)}) %collective-permute-start.5) | collective-permute-done | bytes 45088 | tf_op jit(solution)/shard_map/ppermute | solution.py:10
  108.0 0.1 collective-permute-start.1
  108.2 0.7 collective-permute-done.3
  109.0 0.1 broadcast_select_fusion.7
  109.1 1.7 broadcast_select_fusion.1
  110.9 4.2 %broadcast_select_fusion.5 = (bf16[352,2048]{1,0:T(8,128)(2,1)}, bf16[352,2048]{1,0:T(8,128)(2,1)}) fusion(bf16[352,2048]{1,0:T(8,128)(2,1)} %collective-permute-done, pred[]{:T(512)S(6)} %eq.65, bf16[1,352,2048]{2,1,0:T(8,128)(2,1)S(1)} %copy-done.10), kind=kLoop, calls=%fused_computation.26 | loop fusion | flops 1441792 | bytes 5767169 | tf_op jit(solution)/shard_map/jit(_where)/select_n | solution.py:37
  115.2 1.3 broadcast_select_fusion.3
  116.5 3.8 %convolution_convert_fusion.2 = bf16[896,128]{0,1:T(8,128)(2,1)S(1)} fusion(bf16[896,2048]{1,0:T(8,128)(2,1)} %bitcast.5, bf16[1024,128]{0,1:T(8,128)(2,1)S(1)} %get-tuple-element.14, bf16[1024,128]{0,1:T(8,128)(2,1)S(1)} %get-tuple-element.13), kind=kOutput, calls=%fused_computation.27 | convolution fusion | flops 470925312 | bytes 4423680 | tf_op jit(solution)/shard_map/dot_general | solution.py:52
  120.3 0.6 fusion.16
  121.0 2.1 fusion.19
  123.1 6.8 %fusion.9 = f32[896,704]{0,1:T(8,128)} fusion(f32[896,704]{0,1:T(8,128)S(1)} %fusion.16, bf16[896,2048]{1,0:T(8,128)(2,1)} %bitcast.5, bf16[2048,352]{0,1:T(8,128)(2,1)S(1)} %get-tuple-element.10, bf16[2048,352]{0,1:T(8,128)(2,1)S(1)} %get-tuple-element.9), kind=kOutput, calls=%fused_computation.20 | convolution fusion | flops 2590089216 | bytes 11599872 | tf_op jit(solution)/shard_map/dot_general | solution.py:55
  129.9 50.6 %all-to-all-done = bf16[16,56,2048]{2,1,0:T(8,128)(2,1)} async-done(((bf16[16,56,2048]{2,1,0:T(8,128)(2,1)}), bf16[16,56,2048]{2,1,0:T(8,128)(2,1)}, u32[]{:S(2)}, u32[]{:S(2)}) %all-to-all-start) | async-done | bytes 3670048 | tf_op jit(solution)/shard_map/all_to_all | solution.py:119
  180.5 7.1 %multiply_convert_fusion.1 = (bf16[896,704]{0,1:T(8,128)(2,1)S(1)}, f32[896,704]{0,1:T(8,128)S(1)}) fusion(f32[896,704]{0,1:T(8,128)} %fusion.9, bf16[896,2048]{1,0:T(8,128)(2,1)} %bitcast.2, bf16[352,2048]{1,0:T(8,128)(2,1)} %get-tuple-element.8, bf16[352,2048]{1,0:T(8,128)(2,1)} %get-tuple-element.7), kind=kOutput, calls=%fused_computation.12 | convolution fusion | flops 2593243136 | bytes 12861440 | tf_op jit(solution)/shard_map/dot_general | solution.py:24
  187.6 0.4 convolution_convert_fusion.3
  188.0 3.1 %fusion.7 = f32[896,2048]{1,0:T(8,128)S(1)} fusion(bf16[896,704]{0,1:T(8,128)(2,1)S(1)} %get-tuple-element.21, bf16[2048,352]{0,1:T(8,128)(2,1)S(1)} %copy-done.7, bf16[2048,352]{0,1:T(8,128)(2,1)S(1)} %get-tuple-element.5), kind=kOutput, calls=%fused_computation.18 | convolution fusion | flops 2589458432 | bytes 11485184 | tf_op jit(solution)/shard_map/dot_general | solution.py:24
  191.1 6.7 %multiply_convert_fusion.2 = bf16[896,704]{0,1:T(8,128)(2,1)S(1)} fusion(f32[896,704]{0,1:T(8,128)S(1)} %copy-done.24, f32[896,704]{0,1:T(8,128)S(1)} %get-tuple-element.22, f32[896,704]{0,1:T(8,128)S(1)} %copy-done.8, bf16[896,2048]{1,0:T(8,128)(2,1)} %bitcast.5, bf16[2048,352]{0,1:T(8,128)(2,1)S(1)} %copy-done.7, bf16[2048,352]{0,1:T(8,128)(2,1)} %copy-done.6), kind=kOutput, calls=%fused_computation.13 | convolution fusion | flops 2596397056 | bytes 15384576 | tf_op jit(solution)/shard_map/dot_general | solution.py:58
  197.8 0.4 convolution_convert_fusion.4
  198.2 3.1 %fusion.5 = f32[896,2048]{1,0:T(8,128)S(1)} fusion(bf16[896,704]{0,1:T(8,128)(2,1)S(1)} %multiply_convert_fusion.2, bf16[2048,352]{0,1:T(8,128)(2,1)S(1)} %copy-done.5, bf16[2048,352]{0,1:T(8,128)(2,1)S(1)} %copy-done.3), kind=kOutput, calls=%fused_computation.16 | convolution fusion | flops 2589458432 | bytes 11485184 | tf_op jit(solution)/shard_map/dot_general | solution.py:24
  201.3 3.1 %add_convert_fusion = bf16[896,2048]{1,0:T(8,128)(2,1)} fusion(f32[896,2048]{1,0:T(8,128)S(1)} %fusion.5, f32[896,2048]{1,0:T(8,128)S(1)} %fusion.7, bf16[1024,128]{0,1:T(8,128)(2,1)S(1)} %get-tuple-element.14, bf16[1024,128]{0,1:T(8,128)(2,1)S(1)} %get-tuple-element.13, bf16[896,64]{0,1:T(8,128)(2,1)S(1)} %convolution_convert_fusion.3, ...), kind=kOutput, calls=%fused_computation | convolution fusion | flops 476774400 | bytes 19103744 | tf_op jit(solution)/shard_map/dot_general | solution.py:24
  204.4 9.2 %all-to-all-start.2 = ((bf16[16,56,2048]{2,1,0:T(8,128)(2,1)}), bf16[16,56,2048]{2,1,0:T(8,128)(2,1)}, u32[]{:S(2)}, u32[]{:S(2)}) async-start(bf16[16,56,2048]{2,1,0:T(8,128)(2,1)} %bitcast.69), calls=%async_computation.2 | async-start | bytes 7340032 | tf_op jit(solution)/shard_map/all_to_all | solution.py:119
  213.6 0.5 convolution_bitcast_fusion.1
  214.1 1.4 convolution_bitcast_fusion
  215.5 0.1 fusion.11
  215.7 2.8 fusion.14
  218.6 0.6 collective-permute-start.6
  219.1 0.1 fusion.13
  219.2 0.7 fusion.37
  219.9 0.7 collective-permute-done.6
  220.7 0.8 slice_bitcast_fusion
  221.6 69.2 %all-to-all-done.2 = bf16[16,56,2048]{2,1,0:T(8,128)(2,1)} async-done(((bf16[16,56,2048]{2,1,0:T(8,128)(2,1)}), bf16[16,56,2048]{2,1,0:T(8,128)(2,1)}, u32[]{:S(2)}, u32[]{:S(2)}) %all-to-all-start.2) | async-done | bytes 3670048 | tf_op jit(solution)/shard_map/all_to_all | solution.py:119
  290.8 3.6 %convolution_convert_fusion.1 = bf16[128,2048]{1,0:T(8,128)(2,1)} fusion(pred[896,128]{1,0:T(8,128)(4,1)S(1)} %fusion.4, bf16[896,2048]{1,0:T(8,128)(2,1)} %bitcast.13), kind=kOutput, calls=%fused_computation.15 | convolution fusion | flops 470024192 | bytes 4308992 | tf_op jit(solution)/shard_map/dot_general | solution.py:30
  (67 shorter events, 0.8 us)
Async XLA Ops:
  0.6 4.6 %copy-start = (bf16[128,2048]{1,0:T(8,128)(2,1)S(1)}, bf16[128,2048]{1,0:T(8,128)(2,1)}, u32[]{:S(2)}) copy-start(bf16[128,2048]{1,0:T(8,128)(2,1)} %param.11) | copy-start | bytes 1572868
  8.3 7.1 %copy-start.23 = (f32[128,6]{0,1:T(8,128)S(1)}, f32[128,6]{0,1:T(8,128)}, u32[]{:S(2)}) copy-start(f32[128,6]{0,1:T(8,128)} %param.14) | copy-start | bytes 9220
  8.3 7.5 %copy-start.14 = (bf16[128,2048]{1,0:T(8,128)(2,1)S(1)}, bf16[128,2048]{1,0:T(8,128)(2,1)}, u32[]{:S(2)}) copy-start(bf16[128,2048]{1,0:T(8,128)(2,1)} %param.12) | copy-start | bytes 1572868
  8.3 85.3 %all-to-all-start.1 = ((bf16[16,56,2048]{2,1,0:T(8,128)(2,1)}), bf16[16,56,2048]{2,1,0:T(8,128)(2,1)}, u32[]{:S(2)}, u32[]{:S(2)}) async-start(bf16[16,56,2048]{2,1,0:T(8,128)(2,1)} %bitcast.68), calls=%async_computation.1 | async-start | bytes 7340032 | tf_op jit(solution)/shard_map/all_to_all | solution.py:119
  93.6 9.7 %copy-start.9 = (bf16[1,2048,352]{1,2,0:T(8,128)(2,1)S(1)}, bf16[1,2048,352]{1,2,0:T(8,128)(2,1)}, u32[]{:S(2)}) copy-start(bf16[1,2048,352]{1,2,0:T(8,128)(2,1)} %param.15) | copy-start | bytes 4325380
  93.6 10.3 %copy-start.21 = (bf16[1,64,352]{2,1,0:T(8,128)(2,1)S(1)}, bf16[1,64,352]{2,1,0:T(8,128)(2,1)}, u32[]{:S(2)}) copy-start(bf16[1,64,352]{2,1,0:T(8,128)(2,1)} %param.19) | copy-start | bytes 135172
  93.6 10.4 %copy-start.15 = (bf16[1,1024,64]{1,2,0:T(8,128)(2,1)S(1)}, bf16[1,1024,64]{1,2,0:T(8,128)(2,1)}, u32[]{:S(2)}) copy-start(bf16[1,1024,64]{1,2,0:T(8,128)(2,1)} %param.20) | copy-start | bytes 393220
  93.6 10.4 %copy-start.16 = (bf16[1,1024,64]{1,2,0:T(8,128)(2,1)S(1)}, bf16[1,1024,64]{1,2,0:T(8,128)(2,1)}, u32[]{:S(2)}) copy-start(bf16[1,1024,64]{1,2,0:T(8,128)(2,1)} %param.18) | copy-start | bytes 393220
  93.6 10.9 %copy-start.22 = (bf16[1,64,352]{2,1,0:T(8,128)(2,1)S(1)}, bf16[1,64,352]{2,1,0:T(8,128)(2,1)}, u32[]{:S(2)}) copy-start(bf16[1,64,352]{2,1,0:T(8,128)(2,1)} %param.21) | copy-start | bytes 135172
  93.7 86.8 %all-to-all-start = ((bf16[16,56,2048]{2,1,0:T(8,128)(2,1)}), bf16[16,56,2048]{2,1,0:T(8,128)(2,1)}, u32[]{:S(2)}, u32[]{:S(2)}) async-start(bf16[16,56,2048]{2,1,0:T(8,128)(2,1)} %bitcast.70), calls=%async_computation | async-start | bytes 7340032 | tf_op jit(solution)/shard_map/all_to_all | solution.py:119
  103.3 5.8 %collective-permute-start.4 = (bf16[2048,352]{0,1:T(8,128)(2,1)S(1)}, bf16[2048,352]{0,1:T(8,128)(2,1)}, u32[]{:S(2)}, u32[]{:S(2)}) collective-permute-start(bf16[2048,352]{0,1:T(8,128)(2,1)S(1)} %bitcast.71), channel_id=1, source_target_pairs={{0,1},{1,0},{2,3},{3,2},{4,5},{5,4},{6,7},{7,6},{8,9},{9,8},{10,11... | collective-permute-start | bytes 4325384 | tf_op jit(solution)/shard_map/ppermute | solution.py:10
  103.4 7.4 %collective-permute-start = (bf16[352,2048]{1,0:T(8,128)(2,1)}, bf16[352,2048]{1,0:T(8,128)(2,1)}, u32[]{:S(2)}, u32[]{:S(2)}) collective-permute-start(bf16[352,2048]{1,0:T(8,128)(2,1)} %bitcast.72), channel_id=1, source_target_pairs={{0,1},{1,0},{2,3},{3,2},{4,5},{5,4},{6,7},{7,6},{8,9},{9,8},{10,11... | collective-permute-start | bytes 4325384 | tf_op jit(solution)/shard_map/ppermute | solution.py:10
  103.9 4.1 %collective-permute-start.5 = (bf16[64,352]{1,0:T(8,128)(2,1)S(1)}, bf16[64,352]{1,0:T(8,128)(2,1)S(1)}, u32[]{:S(2)}, u32[]{:S(2)}) collective-permute-start(bf16[64,352]{1,0:T(8,128)(2,1)S(1)} %bitcast.78), channel_id=1, source_target_pairs={{0,1},{1,0},{2,3},{3,2},{4,5},{5,4},{6,7},{7,6},{8,9},{9,8},{10,11... | collective-permute-start | bytes 135176 | tf_op jit(solution)/shard_map/ppermute | solution.py:10
  104.0 4.9 %collective-permute-start.2 = (bf16[1024,128]{0,1:T(8,128)(2,1)S(1)}, bf16[1024,128]{0,1:T(8,128)(2,1)S(1)}, u32[]{:S(2)}, u32[]{:S(2)}) collective-permute-start(bf16[1024,128]{0,1:T(8,128)(2,1)S(1)} %pad_maximum_fusion.15), channel_id=1, source_target_pairs={{0,1},{1,0},{2,3},{3,2},{4,5},{5,4},{6,7},{7,6},{8,9},{9,8},{10,11... | collective-permute-start | bytes 786440 | tf_op jit(solution)/shard_map/ppermute | solution.py:10
  104.5 4.4 %collective-permute-start.3 = (bf16[64,352]{1,0:T(8,128)(2,1)S(1)}, bf16[64,352]{1,0:T(8,128)(2,1)S(1)}, u32[]{:S(2)}, u32[]{:S(2)}) collective-permute-start(bf16[64,352]{1,0:T(8,128)(2,1)S(1)} %bitcast.79), channel_id=1, source_target_pairs={{0,1},{1,0},{2,3},{3,2},{4,5},{5,4},{6,7},{7,6},{8,9},{9,8},{10,11... | collective-permute-start | bytes 135176 | tf_op jit(solution)/shard_map/ppermute | solution.py:10
  108.0 7.1 %collective-permute-start.1 = (bf16[2048,352]{0,1:T(8,128)(2,1)}, bf16[2048,352]{0,1:T(8,128)(2,1)S(1)}, u32[]{:S(2)}, u32[]{:S(2)}) collective-permute-start(bf16[2048,352]{0,1:T(8,128)(2,1)} %bitcast.73), channel_id=1, source_target_pairs={{0,1},{1,0},{2,3},{3,2},{4,5},{5,4},{6,7},{7,6},{8,9},{9,8},{10,11... | collective-permute-start | bytes 4325384 | tf_op jit(solution)/shard_map/ppermute | solution.py:10
  108.9 12.0 %copy-start.17 = (bf16[64,352]{1,0:T(8,128)(2,1)}, bf16[64,352]{1,0:T(8,128)(2,1)S(1)}, u32[]{:S(2)}) copy-start(bf16[64,352]{1,0:T(8,128)(2,1)S(1)} %get-tuple-element.17) | copy-start | bytes 135172
  109.0 12.0 %copy-start.19 = (bf16[64,352]{1,0:T(8,128)(2,1)}, bf16[64,352]{1,0:T(8,128)(2,1)S(1)}, u32[]{:S(2)}) copy-start(bf16[64,352]{1,0:T(8,128)(2,1)S(1)} %get-tuple-element.18) | copy-start | bytes 135172
  109.1 1.8 copy-start.10
  110.8 12.3 %copy-start.2 = (bf16[2048,352]{0,1:T(8,128)(2,1)}, bf16[2048,352]{0,1:T(8,128)(2,1)S(1)}, u32[]{:S(2)}) copy-start(bf16[2048,352]{0,1:T(8,128)(2,1)S(1)} %get-tuple-element.9) | copy-start | bytes 4325380
  110.8 12.3 %copy-start.4 = (bf16[2048,352]{0,1:T(8,128)(2,1)}, bf16[2048,352]{0,1:T(8,128)(2,1)S(1)}, u32[]{:S(2)}) copy-start(bf16[2048,352]{0,1:T(8,128)(2,1)S(1)} %get-tuple-element.10) | copy-start | bytes 4325380
  110.8 4.3 %copy-start.11 = (bf16[1,2048,352]{1,2,0:T(8,128)(2,1)S(1)}, bf16[1,2048,352]{1,2,0:T(8,128)(2,1)}, u32[]{:S(2)}) copy-start(bf16[1,2048,352]{1,2,0:T(8,128)(2,1)} %param.16) | copy-start | bytes 4325380
  116.5 71.5 %copy-start.6 = (bf16[2048,352]{0,1:T(8,128)(2,1)}, bf16[2048,352]{0,1:T(8,128)(2,1)S(1)}, u32[]{:S(2)}) copy-start(bf16[2048,352]{0,1:T(8,128)(2,1)S(1)} %get-tuple-element.5) | copy-start | bytes 4325380
  120.3 2.8 copy-start.12
  180.5 7.1 %copy-start.18 = (bf16[64,352]{1,0:T(8,128)(2,1)S(1)}, bf16[64,352]{1,0:T(8,128)(2,1)}, u32[]{:S(2)}) copy-start(bf16[64,352]{1,0:T(8,128)(2,1)} %copy-done.17) | copy-start | bytes 135172
  180.5 7.1 %copy-start.20 = (bf16[64,352]{1,0:T(8,128)(2,1)S(1)}, bf16[64,352]{1,0:T(8,128)(2,1)}, u32[]{:S(2)}) copy-start(bf16[64,352]{1,0:T(8,128)(2,1)} %copy-done.19) | copy-start | bytes 135172
  180.5 7.5 %copy-start.7 = (bf16[2048,352]{0,1:T(8,128)(2,1)S(1)}, bf16[2048,352]{0,1:T(8,128)(2,1)}, u32[]{:S(2)}) copy-start(bf16[2048,352]{0,1:T(8,128)(2,1)} %get-tuple-element.6) | copy-start | bytes 4325380
  188.0 3.1 %copy-start.8 = (f32[896,704]{0,1:T(8,128)S(1)}, f32[896,704]{0,1:T(8,128)}, u32[]{:S(2)}) copy-start(f32[896,704]{0,1:T(8,128)} %fusion.19) | copy-start | bytes 7569412
  188.0 3.1 %copy-start.24 = (f32[896,704]{0,1:T(8,128)S(1)}, f32[896,704]{0,1:T(8,128)}, u32[]{:S(2)}) copy-start(f32[896,704]{0,1:T(8,128)} %fusion.9) | copy-start | bytes 7569412
  191.1 7.1 %copy-start.3 = (bf16[2048,352]{0,1:T(8,128)(2,1)S(1)}, bf16[2048,352]{0,1:T(8,128)(2,1)}, u32[]{:S(2)}) copy-start(bf16[2048,352]{0,1:T(8,128)(2,1)} %copy-done.2) | copy-start | bytes 4325380
  191.1 7.1 %copy-start.5 = (bf16[2048,352]{0,1:T(8,128)(2,1)S(1)}, bf16[2048,352]{0,1:T(8,128)(2,1)}, u32[]{:S(2)}) copy-start(bf16[2048,352]{0,1:T(8,128)(2,1)} %copy-done.4) | copy-start | bytes 4325380
  204.4 9.2 %copy-start.13 = (bf16[896,128]{0,1:T(8,128)(2,1)S(1)}, bf16[896,128]{0,1:T(8,128)(2,1)}, u32[]{:S(2)}) copy-start(bf16[896,128]{0,1:T(8,128)(2,1)} %copy-done.12) | copy-start | bytes 688132
  204.4 86.4 %all-to-all-start.2 = ((bf16[16,56,2048]{2,1,0:T(8,128)(2,1)}), bf16[16,56,2048]{2,1,0:T(8,128)(2,1)}, u32[]{:S(2)}, u32[]{:S(2)}) async-start(bf16[16,56,2048]{2,1,0:T(8,128)(2,1)} %bitcast.69), calls=%async_computation.2 | async-start | bytes 7340032 | tf_op jit(solution)/shard_map/all_to_all | solution.py:119
  215.7 3.5 %collective-permute-start.7 = (f32[2,64,352]{2,1,0:T(8,128)S(1)}, f32[2,64,352]{2,1,0:T(8,128)S(1)}, u32[]{:S(2)}, u32[]{:S(2)}) collective-permute-start(f32[2,64,352]{2,1,0:T(8,128)S(1)} %fusion.11), channel_id=1, source_target_pairs={{0,1},{1,0},{2,3},{3,2},{4,5},{5,4},{6,7},{7,6},{8,9},{9,8},{10,11... | collective-permute-start | bytes 540680 | tf_op jit(solution)/shard_map/ppermute | solution.py:10
  218.6 2.1 collective-permute-start.6
  220.7 73.7 %copy-start.1 = (bf16[128,2048]{1,0:T(8,128)(2,1)S(1)}, bf16[128,2048]{1,0:T(8,128)(2,1)}, u32[]{:S(2)}) copy-start(bf16[128,2048]{1,0:T(8,128)(2,1)} %param.11) | copy-start | bytes 1572868

commit v2 on v1

v2 whole, which is shorter than its diff:
```python
import functools

import jax
import jax.numpy as jnp
from jax import lax
from jax.experimental import pallas as pl
from jax.experimental.pallas import tpu as pltpu
from jax.sharding import PartitionSpec as P

PLANE = 4
ANY = pl.BlockSpec(memory_space=pl.ANY)
VMEM = pl.BlockSpec(memory_space=pltpu.VMEM)


def trans_right(left, right):
    return lax.dot_general(
        left, right, (((1,), (1,)), ((), ())), preferred_element_type=jnp.float32
    )


def trans_left(left, right):
    return lax.dot_general(
        left, right, (((0,), (0,)), ((), ())), preferred_element_type=jnp.float32
    )


def position(planes):
    me = lax.axis_index("expert")
    half = lax.rem(me, 2)
    chip = lax.div(me, 2)
    return lax.div(chip, PLANE), lax.rem(chip, PLANE), half


def device(z, q, half):
    return {"expert": (z * PLANE + q) * 2 + half}


def remote(src, dst, send, recv, target):
    return pltpu.make_async_remote_copy(
        src_ref=src,
        dst_ref=dst,
        send_sem=send,
        recv_sem=recv,
        device_id=target,
        device_id_type=pl.DeviceIdType.MESH,
    )


def greet(target):
    pl.semaphore_signal(
        pltpu.get_barrier_semaphore(),
        inc=1,
        device_id=target,
        device_id_type=pl.DeviceIdType.MESH,
    )


def dispatch_kernel(
    planes,
    experts,
    cap,
    x_ref,
    c_ref,
    meta_ref,
    *refs,
):
    pieces = refs[:5]
    rows_ref, metas_ref = refs[5:7]
    others = refs[7:12]
    zbuf, zmeta, stage, load_sem, w_send, w_recv = refs[12:18]
    up_send, down_send, z_recv, um_send, dm_send, m_recv, p_send, p_recv, own_sem = refs[18:]
    z, q, half = position(planes)
    tok, width = x_ref.shape
    last = planes - 1

    own_x = pltpu.make_async_copy(x_ref, zbuf.at[z, pl.ds(0, tok)], load_sem.at[0])
    own_c = pltpu.make_async_copy(c_ref, zbuf.at[z, pl.ds(tok, tok)], load_sem.at[1])
    own_x.start()
    own_c.start()
    zmeta[z] = meta_ref[...]

    greet(device(z, q, 1 - half))
    for step in range(1, PLANE):
        greet(device(z, lax.rem(q + step, PLANE), half))

    @pl.when(z < last)
    def _():
        greet(device(z + 1, q, half))

    @pl.when(z > 0)
    def _():
        greet(device(z - 1, q, half))

    near = jnp.where(z < last, 1, 0) + jnp.where(z > 0, 1, 0)
    pl.semaphore_wait(pltpu.get_barrier_semaphore(), PLANE + near)
    own_x.wait()
    own_c.wait()

    def up(b):
        target = device(z + 1, q, half)
        return (
            remote(zmeta.at[b], zmeta.at[b], um_send.at[b], m_recv.at[b], target),
            remote(zbuf.at[b], zbuf.at[b], up_send.at[b], z_recv.at[b], target),
        )

    def down(b):
        target = device(z - 1, q, half)
        return (
            remote(zmeta.at[b], zmeta.at[b], dm_send.at[b], m_recv.at[b], target),
            remote(zbuf.at[b], zbuf.at[b], down_send.at[b], z_recv.at[b], target),
        )

    def begin(copies):
        for copy in copies:
            copy.start()

    def arrived(copies):
        for copy in copies:
            copy.wait_recv()

    def sent(copies):
        for copy in copies:
            copy.wait_send()

    def piece(i):
        return remote(
            pieces[i], others[i], w_send.at[i], w_recv.at[i], device(z, q, 1 - half)
        )

    def part(b, to):
        return remote(
            stage.at[b, to],
            rows_ref.at[q, b],
            p_send.at[b, to],
            p_recv.at[q, b],
            device(z, to, half),
        )

    def came(b, source):
        return remote(
            stage.at[b, source],
            rows_ref.at[source, b],
            p_send.at[b, source],
            p_recv.at[source, b],
            device(z, source, half),
        )

    def local(b):
        return pltpu.make_async_copy(stage.at[b, q], rows_ref.at[q, b], own_sem.at[b])

    def picked(b, to):
        expert = z * PLANE + to
        slots = zmeta[b, pl.ds(expert, 1), :]
        weights = zmeta[b, pl.ds(experts + expert, 1), :]
        numbers = lax.broadcasted_iota(jnp.int32, (cap, tok), 0).astype(jnp.float32)
        mask = numbers == slots
        ones = jnp.where(mask, 1.0, 0.0)
        zeros = jnp.zeros_like(ones)
        scale = jnp.sum(jnp.where(mask, weights, 0.0), axis=1, keepdims=True)
        scale = jnp.concatenate([jnp.ones_like(scale), scale], axis=0)
        picker = jnp.concatenate(
            [
                jnp.concatenate([ones, zeros], axis=1),
                jnp.concatenate([zeros, ones], axis=1),
            ],
            axis=0,
        ).astype(jnp.bfloat16)
        tile = width // 4
        for n in range(4):
            cols = pl.ds(n * tile, tile)
            rows = jnp.dot(picker, zbuf[b, :, cols], preferred_element_type=jnp.float32)
            stage[b, to, :, cols] = (rows * scale).astype(jnp.bfloat16)

    def spread(b):
        def one(step, carry):
            to = lax.rem(q + step, PLANE)
            picked(b, to)
            part(b, to).start()
            return carry

        lax.fori_loop(1, PLANE, one, 0)
        picked(b, q)
        local(b).start()

    @pl.when(z < last)
    def _():
        begin(up(z))

    @pl.when(z > 0)
    def _():
        begin(down(z))

    for i in range(5):
        piece(i).start()
    spread(z)

    def step(k, carry):
        below, above = z - k, z + k

        @pl.when(below >= 0)
        def _():
            arrived(down(below))

            @pl.when(z < last)
            def _():
                begin(up(below))

        @pl.when(above <= last)
        def _():
            arrived(up(above))

            @pl.when(z > 0)
            def _():
                begin(down(above))

        @pl.when(below >= 0)
        def _():
            spread(below)

        @pl.when(above <= last)
        def _():
            spread(above)

        return carry

    lax.fori_loop(1, planes, step, 0)
    metas_ref[...] = zmeta[...]

    def finish(b, carry):
        def one(step, inner):
            to = lax.rem(q + step, PLANE)
            part(b, to).wait_send()
            came(b, to).wait_recv()
            return inner

        lax.fori_loop(1, PLANE, one, 0)
        local(b).wait()

        @pl.when((b <= z) & (z < last))
        def _():
            sent(up(b))

        @pl.when((b >= z) & (z > 0))
        def _():
            sent(down(b))

        return carry

    lax.fori_loop(0, planes, finish, 0)
    for i in range(5):
        piece(i).wait()


def dispatch(planes, experts, cap, tokens, cotangent, meta, pieces):
    tok, width = tokens.shape
    bf16, f32 = jnp.bfloat16, jnp.float32
    dma = pltpu.SemaphoreType.DMA
    shape = jax.ShapeDtypeStruct
    return pl.pallas_call(
        functools.partial(dispatch_kernel, planes, experts, cap),
        out_shape=[
            shape((PLANE, planes, 2 * cap, width), bf16),
            shape((planes,) + meta.shape, f32),
        ]
        + [shape(piece.shape, piece.dtype) for piece in pieces],
        in_specs=[ANY, ANY, VMEM] + [ANY] * len(pieces),
        out_specs=[ANY, VMEM] + [ANY] * len(pieces),
        scratch_shapes=[
            pltpu.VMEM((planes, 2 * tok, width), bf16),
            pltpu.VMEM((planes,) + meta.shape, f32),
            pltpu.VMEM((planes, PLANE, 2 * cap, width), bf16),
            dma((2,)),
            dma((len(pieces),)),
            dma((len(pieces),)),
            dma((planes,)),
            dma((planes,)),
            dma((planes,)),
            dma((planes,)),
            dma((planes,)),
            dma((planes,)),
            dma((planes, PLANE)),
            dma((PLANE, planes)),
            dma((planes,)),
        ],
        compiler_params=pltpu.CompilerParams(
            collective_id=0, has_side_effects=True, vmem_limit_bytes=40 * 2**20
        ),
        name="dispatch",
    )(tokens, cotangent, meta, *pieces)


CHUNKS = 4


def combine_kernel(
    planes,
    y_ref,
    pick_ref,
    keep_a,
    give_a,
    keep_b,
    give_b,
    out_ref,
    sum_a,
    sum_b,
    ybuf,
    stage,
    zin,
    got_a,
    got_b,
    y_send,
    y_recv,
    own_sem,
    z_send,
    z_recv,
    g_send,
    g_recv,
):
    z, q, half = position(planes)
    tok, width = out_ref.shape
    tile = width // CHUNKS

    greet(device(z, q, 1 - half))
    for step in range(1, PLANE):
        greet(device(z, lax.rem(q + step, PLANE), half))

    def hello(step, carry):
        greet(device(lax.rem(z + step, planes), q, half))
        return carry

    lax.fori_loop(1, planes, hello, 0)
    pl.semaphore_wait(pltpu.get_barrier_semaphore(), PLANE + planes - 1)

    def cols(j):
        return pl.ds(pl.multiple_of(j * tile, tile), tile)

    def give(j, to):
        return remote(
            y_ref.at[to, :, cols(j)],
            ybuf.at[q, :, cols(j)],
            y_send.at[j, to],
            y_recv.at[j, q],
            device(z, to, half),
        )

    def came(j, source):
        return remote(
            y_ref.at[source, :, cols(j)],
            ybuf.at[source, :, cols(j)],
            y_send.at[j, source],
            y_recv.at[j, source],
            device(z, source, half),
        )

    def local(j):
        return pltpu.make_async_copy(
            y_ref.at[q, :, cols(j)], ybuf.at[q, :, cols(j)], own_sem.at[j]
        )

    def part(j, to):
        return remote(
            stage.at[to, :, cols(j)],
            zin.at[z, :, cols(j)],
            z_send.at[j, to],
            z_recv.at[j, z],
            device(to, q, half),
        )

    def part_came(j, source):
        return remote(
            stage.at[source, :, cols(j)],
            zin.at[source, :, cols(j)],
            z_send.at[j, source],
            z_recv.at[j, source],
            device(source, q, half),
        )

    partner = device(z, q, 1 - half)
    grads = (
        remote(give_a, got_a, g_send.at[0], g_recv.at[0], partner),
        remote(give_b, got_b, g_send.at[1], g_recv.at[1], partner),
    )

    def send(j, carry):
        def one(step, inner):
            give(j, lax.rem(q + step, PLANE)).start()
            return inner

        lax.fori_loop(1, PLANE, one, 0)
        local(j).start()
        return carry

    lax.fori_loop(0, CHUNKS, send, 0)
    for copy in grads:
        copy.start()

    def work(j, carry):
        def one(step, inner):
            came(j, lax.rem(q + step, PLANE)).wait_recv()
            return inner

        lax.fori_loop(1, PLANE, one, 0)
        local(j).wait()
        for target in range(planes):
            rows = pl.ds(target * tok, tok)
            total = jnp.zeros((tok, tile), jnp.float32)
            for source in range(PLANE):
                total += jnp.dot(
                    pick_ref[source, rows, :],
                    ybuf[source, :, cols(j)],
                    preferred_element_type=jnp.float32,
                )
            stage[target, :, cols(j)] = total.astype(jnp.bfloat16)

        def post(step, inner):
            part(j, lax.rem(z + step, planes)).start()
            return inner

        lax.fori_loop(1, planes, post, 0)
        return carry

    lax.fori_loop(0, CHUNKS, work, 0)

    for copy in grads:
        copy.wait()
    sum_a[...] = keep_a[...] + got_a[...]
    sum_b[...] = keep_b[...] + got_b[...]

    def gather(j, carry):
        def one(step, total):
            source = lax.rem(z + step, planes)
            part_came(j, source).wait_recv()
            return total + zin[source, :, cols(j)].astype(jnp.float32)

        total = lax.fori_loop(1, planes, one, stage[z, :, cols(j)].astype(jnp.float32))
        out_ref[:, cols(j)] = total.astype(jnp.bfloat16)
        return carry

    lax.fori_loop(0, CHUNKS, gather, 0)

    def finish(j, carry):
        def one(step, inner):
            give(j, lax.rem(q + step, PLANE)).wait_send()
            return inner

        def two(step, inner):
            part(j, lax.rem(z + step, planes)).wait_send()
            return inner

        lax.fori_loop(1, PLANE, one, 0)
        lax.fori_loop(1, planes, two, 0)
        return carry

    lax.fori_loop(0, CHUNKS, finish, 0)


def combine(planes, tok, y, pick, keep_a, give_a, keep_b, give_b):
    width = y.shape[2]
    bf16, f32 = jnp.bfloat16, jnp.float32
    dma = pltpu.SemaphoreType.DMA
    shape = jax.ShapeDtypeStruct
    return pl.pallas_call(
        functools.partial(combine_kernel, planes),
        out_shape=[
            shape((tok, width), bf16),
            shape(keep_a.shape, f32),
            shape(keep_b.shape, f32),
        ],
        in_specs=[ANY, VMEM, VMEM, VMEM, VMEM, VMEM],
        out_specs=[VMEM, VMEM, VMEM],
        scratch_shapes=[
            pltpu.VMEM(y.shape, bf16),
            pltpu.VMEM((planes, tok, width), bf16),
            pltpu.VMEM((planes, tok, width), bf16),
            pltpu.VMEM(keep_a.shape, f32),
            pltpu.VMEM(keep_b.shape, f32),
            dma((CHUNKS, PLANE)),
            dma((CHUNKS, PLANE)),
            dma((CHUNKS,)),
            dma((CHUNKS, planes)),
            dma((CHUNKS, planes)),
            dma((2,)),
            dma((2,)),
        ],
        compiler_params=pltpu.CompilerParams(
            collective_id=1, has_side_effects=True, vmem_limit_bytes=40 * 2**20
        ),
        name="combine",
    )(y, pick, keep_a, give_a, keep_b, give_b)


def expert_rows(rows_x, rows_dy, own, other, my_half):
    adapter_own, adapter_other = own[3], other[3]
    rank = own[4].shape[0] // 2
    adapters = jnp.where(
        my_half == 0,
        jnp.concatenate([adapter_own, adapter_other], axis=0),
        jnp.concatenate([adapter_other, adapter_own], axis=0),
    )
    low_rank = jnp.dot(rows_x, adapters, preferred_element_type=jnp.float32).astype(jnp.bfloat16)
    low_gate = low_rank[:, :rank]
    low_up = low_rank[:, rank:]
    row_grads = 0.0
    back = 0.0
    grads_b = []
    for gate_w, up_w, down_w, _, b_out in (own, other):
        b_gate, b_up = b_out[:rank], b_out[rank:]
        gate = jnp.dot(rows_x, gate_w, preferred_element_type=jnp.float32) + jnp.dot(
            low_gate, b_gate, preferred_element_type=jnp.float32
        )
        upward = jnp.dot(rows_x, up_w, preferred_element_type=jnp.float32) + jnp.dot(
            low_up, b_up, preferred_element_type=jnp.float32
        )
        hidden_grad = trans_right(rows_dy, down_w)
        sigmoid_gate = jax.nn.sigmoid(gate)
        grad_gate = (
            hidden_grad * upward * sigmoid_gate * (1.0 + gate * (1.0 - sigmoid_gate))
        ).astype(jnp.bfloat16)
        grad_up = (hidden_grad * gate * sigmoid_gate).astype(jnp.bfloat16)
        back += jnp.concatenate(
            [trans_right(grad_gate, b_gate), trans_right(grad_up, b_up)], axis=1
        )
        row_grads += trans_right(grad_gate, gate_w) + trans_right(grad_up, up_w)
        grads_b.append(jnp.stack([trans_left(low_gate, grad_gate), trans_left(low_up, grad_up)]))
    back = back.astype(jnp.bfloat16)
    row_grads = (row_grads + trans_right(back, adapters)).astype(jnp.bfloat16)
    return row_grads, trans_left(rows_x, back), grads_b


def on_device(
    tokens,
    cotangent,
    token_experts,
    routing_weight_cache,
    gate_weight,
    up_weight,
    down_weight,
    gate_adapter_input,
    gate_adapter_output,
    up_adapter_input,
    up_adapter_output,
):
    n_devices = lax.axis_size("expert")
    n_experts = n_devices // 2
    planes = n_experts // PLANE
    tok, width = tokens.shape
    top = token_experts.shape[1]
    rank = gate_adapter_input.shape[2]
    slot_cap = 2 * max(2, 9 * tok * top // (16 * n_experts) + 1)
    slot_cap = (slot_cap + 7) // 8 * 8
    my_z, _, my_half = position(planes)

    named = token_experts[None, :, :] == jnp.arange(n_experts, dtype=jnp.int32)[:, None, None]
    chosen = jnp.any(named, axis=2).astype(jnp.float32)
    earlier = (
        lax.broadcasted_iota(jnp.int32, (tok, tok), 0)
        < lax.broadcasted_iota(jnp.int32, (tok, tok), 1)
    ).astype(jnp.float32)
    slots = jnp.dot(chosen, earlier, preferred_element_type=jnp.float32)
    slots = jnp.where(chosen > 0, slots, -1.0)
    weights = jnp.sum(jnp.where(named, routing_weight_cache[None, :, :], 0.0), axis=2)
    meta = jnp.concatenate([slots, weights], axis=0)

    own = (
        gate_weight[0],
        up_weight[0],
        down_weight[0],
        jnp.concatenate([gate_adapter_input[0], up_adapter_input[0]], axis=1),
        jnp.concatenate([gate_adapter_output[0], up_adapter_output[0]], axis=0),
    )
    rows, metas, *other = dispatch(planes, n_experts, slot_cap, tokens, cotangent, meta, own)
    rows_x = rows[:, :, :slot_cap].reshape(-1, width)
    rows_dy = rows[:, :, slot_cap:].reshape(-1, width)
    row_grads, grad_a, grads_b = expert_rows(rows_x, rows_dy, own, other, my_half)

    plane_slots = lax.dynamic_slice_in_dim(metas, my_z * PLANE, PLANE, 1)
    same = jnp.eye(planes, dtype=jnp.bool_)[None, :, None, :, None]
    hit = plane_slots.transpose(1, 0, 2)[:, :, :, None, None] == jnp.arange(
        slot_cap, dtype=jnp.float32
    )
    pick = (same & hit).astype(jnp.bfloat16).reshape(PLANE, planes * tok, planes * slot_cap)

    half_width = grad_a.shape[0] // 2
    keep_a = lax.dynamic_slice_in_dim(grad_a, my_half * half_width, half_width, 0)
    give_a = lax.dynamic_slice_in_dim(grad_a, (1 - my_half) * half_width, half_width, 0)
    grad_tokens, sum_a, sum_b = combine(
        planes,
        tok,
        row_grads.reshape(PLANE, planes * slot_cap, width),
        pick,
        keep_a,
        give_a,
        grads_b[0],
        grads_b[1],
    )
    return (
        grad_tokens,
        sum_a[None, :, :rank],
        sum_b[None, 0],
        sum_a[None, :, rank:],
        sum_b[None, 1],
    )


def solution(mesh):
    in_specs = (
        P(("groups", "expert"), None),
        P(("groups", "expert"), None),
        P(("groups", "expert"), None),
        P(("groups", "expert"), None),
        P("expert", None, None),
        P("expert", None, None),
        P("expert", None, None),
        P("expert", None, None),
        P("expert", None, None),
        P("expert", None, None),
        P("expert", None, None),
    )
    out_specs = (
        P(("groups", "expert"), None),
        P(("groups", "expert"), None, None),
        P(("groups", "expert"), None, None),
        P(("groups", "expert"), None, None),
        P(("groups", "expert"), None, None),
    )
    return jax.shard_map(
        on_device, mesh=mesh, in_specs=in_specs, out_specs=out_specs, check_vma=False
    )
```

time: 299 us -> 231 us (0.77); the launches traced: 294 us -> 229 us
  waiting for transfers between devices: 200 us -> 0 us
  Pallas kernels: 0 us -> 156 us
  starting transfers between devices: 28 us -> 0 us
  local copies, waits for them, and re-layouts: 3.3 us -> 24.7 us
  other arithmetic: 11 us -> 0.69 us
  matrix products: 51.4 us -> 47.1 us
    all_to_all x3 -> x0, waiting for transfers between devices: 195 us -> none  [exchanged(): lax.all_to_all(rows.reshape(n_experts, slot_cap, width), 'expert', split_...]
    pallas_call x0 -> x2, Pallas kernels: none -> 156 us  [the longest x1 93.1 us: dispatch(): pl.pallas_call(functools.partial(dispatch_kernel, planes, experts, cap),...]
    all_to_all x3 -> x0, starting transfers between devices: 26 us -> none  [exchanged(): lax.all_to_all(rows.reshape(n_experts, slot_cap, width), 'expert', split_...]
    dot_general x6 -> x11, matrix products: 17.1 us -> 32.9 us  [trans_right(): lax.dot_general(left, right, (((1,), (1,)), ((), ())), preferred_element_...]
    unnamed x51 -> x70, local copies, waits for them, and re-layouts: 1.04 us -> 15.3 us
    select_n x6 -> x0, other arithmetic: 7.35 us -> none  [joined(): first = jnp.where(my_half == 0, own, other)]
    dot_general x2 -> x1, matrix products: 5.98 us -> 0.13 us  [on_device(): slots = jnp.dot(chosen, earlier, preferred_element_type=jnp.float32)]
    ppermute x8 -> x0, waiting for transfers between devices: 4.88 us -> none  [swapped(): return lax.ppermute(value, axis, pairs)]
  transfers between devices with their start and end apart: 11 -> 0, of which waited for: 6 -> 0; matrix products, arithmetic and copies ran while one was open for 10% -> 0% of each run, Pallas kernels for 0% -> 0%
where the time goes in v2:
time: 231 us; the launch traced here: 229 us
  Pallas kernels  156 us (68%)
  matrix products  47.1 us (20%)
  local copies, waits for them, and re-layouts  24.7 us (11%)
    pallas_call x1, Pallas kernels, dispatch(): pl.pallas_call(functools.partial(dispatch_kernel, planes, experts, cap),...  93.1 us
    pallas_call x1, Pallas kernels, combine(): pl.pallas_call(functools.partial(combine_kernel, planes), out_shape=[shap...  62.6 us
    dot_general x11, matrix products, trans_right(): lax.dot_general(left, right, (((1,), (1,)), ((), ())), preferred_element_...  32.9 us
    unnamed x70, local copies, waits for them, and re-layouts  15.3 us
    slice x1, local copies, waits for them, and re-layouts, on_device(): rows_x = rows[:, :, :slot_cap].reshape(-1, width)  5.1 us

profile of v2, /device:TPU:24, one launch (start us, length us, event | category | flops | bytes accessed | tf_op | source)
XLA Modules:
  0.0 229.5 jit_solution(6899599850746820874)
XLA Ops:
  0.7 1.2 copy.38
  1.9 1.2 copy.39
  3.0 0.7 copy-done.21
  3.9 0.9 copy.36
  4.8 1.9 copy.37
  6.9 1.4 copy-done.5
  8.3 1.0 copy-done.7
  9.3 1.0 copy-done.8
  10.4 93.1 %dispatch.1 = (bf16[4,4,112,2048]{3,2,1,0:T(8,128)(2,1)}, f32[4,32,128]{2,1,0:T(8,128)S(1)}, bf16[2048,352]{1,0:T(8,128)(2,1)S(1)}, bf16[2048,352]{1,0:T(8,128)(...) custom-call(bf16[128,2048]{1,0:T(8,128)(2,1)S(1)} %copy-done.7, ...), custom_call_target="tpu_custom_call" | custom-call | tf_op jit(solution)/shard_map/dispatch/pallas_call | solution.py:259
  103.6 5.1 %fusion.40 = (bf16[4,4,56,2048]{3,2,1,0:T(8,128)(2,1)S(1)}, bf16[4,4,56,2048]{3,2,1,0:T(8,128)(2,1)S(1)}) fusion(bf16[4,4,112,2048]{3,2,1,0:T(8,128)(2,1)} %get-tuple-element.15), kind=kLoop, calls=%fused_computation.75 | loop fusion | bytes 14680064 | tf_op jit(solution)/shard_map/slice | solution.py:572
  108.7 1.3 convolution_convert_fusion
  110.1 1.7 fusion.2
  111.8 0.4 convolution_add_fusion.2
  112.2 1.0 copy-done.6
  113.1 1.7 multiply_convert_fusion.1
  114.9 1.7 fusion.6
  116.6 0.7 fusion.14
  117.4 0.3 convolution_bitcast_fusion.3
  117.7 0.3 convolution_bitcast_fusion.2
  118.0 1.7 fusion.43
  119.8 0.4 convolution_add_fusion
  120.1 1.7 multiply_convert_fusion
  121.9 2.0 fusion.42
  123.9 0.7 fusion.15
  124.6 0.3 convolution_bitcast_fusion.1
  124.9 0.3 convolution_bitcast_fusion
  125.3 0.2 fusion.35
  125.5 0.2 fusion.26
  125.8 0.2 fusion.29
  126.3 2.2 fusion.46
  128.5 1.4 constant_dynamic-slice_fusion
  129.9 0.3 copy-done.15
  130.2 2.1 fusion
  132.3 5.1 %fusion.44 = f32[896,2048]{1,0:T(8,128)} fusion(bf16[896,352]{0,1:T(8,128)(2,1)S(1)} %copy-done.12, bf16[2048,352]{1,0:T(8,128)(2,1)S(1)} %copy-done.4), kind=kOutput, calls=%fused_computation.79 | convolution fusion | flops 1291845632 | bytes 9412608 | tf_op jit(solution)/shard_map/dot_general | solution.py:16
  137.4 5.1 %fusion.45 = f32[896,2048]{1,0:T(8,128)} fusion(bf16[896,352]{0,1:T(8,128)(2,1)S(1)} %get-tuple-element.48, bf16[2048,352]{1,0:T(8,128)(2,1)S(1)} %copy-done.2), kind=kOutput, calls=%fused_computation.80 | convolution fusion | flops 1291845632 | bytes 9412608 | tf_op jit(solution)/shard_map/dot_general | solution.py:16
  142.5 5.1 %fusion.4 = f32[896,2048]{1,0:T(8,128)} fusion(bf16[896,352]{0,1:T(8,128)(2,1)S(1)} %get-tuple-element.50, bf16[1,2048,352]{1,2,0:T(8,128)(2,1)S(1)} %copy-done.17), kind=kOutput, calls=%fused_computation.6 | convolution fusion | flops 1291845632 | bytes 9412608 | tf_op jit(solution)/shard_map/dot_general | solution.py:16
  147.6 11.1 %add_convert_fusion = bf16[896,2048]{1,0:T(8,128)(2,1)} fusion(f32[896,2048]{1,0:T(8,128)} %fusion.44, f32[896,2048]{1,0:T(8,128)} %fusion.45, f32[896,2048]{1,0:T(8,128)S(1)} %fusion, f32[896,2048]{1,0:T(8,128)} %fusion.4, bf16[896,128]{0,1:T(8,128)(2,1)S(1)} %copy-done.25, bf16[1024,128]{1,0:T(8,128)(2,1)S(1)} %copy-done.10, ...), kind=kOutput, calls=%fused_computation | convolution fusion | flops 482344960 | bytes 33783808 | tf_op jit(solution)/shard_map/dot_general | solution.py:16
  158.9 0.3 and.25
  159.2 0.4 and.26
  159.6 1.0 copy.42
  160.8 0.3 copy.40
  161.1 0.3 and_convert_fusion.pick_ref
  161.4 2.0 copy-done
  163.4 62.6 %combine.1 = (bf16[128,2048]{1,0:T(8,128)(2,1)S(1)}, f32[1024,128]{1,0:T(8,128)S(1)}, f32[2,64,352]{2,1,0:T(8,128)S(1)}) custom-call(bf16[4,224,2048]{2,1,0:T(8,128)(2,1)S(1)} %bitcast.85, bf16[4,512,224]{2,1,0:T(8,128)(2,1)S(1)} %and_convert_fusion.pick_ref, f32[1024,128]{1,0:T(8,128)S(1)} %get-tuple-element.43.keep_a, ...), custom_call_target="tpu_custom_call" | custom-call | tf_op jit(solution)/shard_map/combine/pallas_call | solution.py:462
  226.2 0.9 copy.43
  227.1 0.9 copy.44
  228.0 0.7 fusion.41
  228.7 0.8 copy.49
  (71 shorter events, 1.3 us)
Async XLA Ops:
  0.6 3.3 %copy-start.13 = (bf16[1,2048,352]{1,2,0:T(8,128)(2,1)S(1)}, bf16[1,2048,352]{1,2,0:T(8,128)(2,1)}, u32[]{:S(2)}) copy-start(bf16[1,2048,352]{1,2,0:T(8,128)(2,1)} %param.15) | copy-start | bytes 4325380
  1.8 1.2 copy-start.18
  3.0 0.7 copy-start.21
  4.8 1.9 copy-start.26
  4.8 1.9 copy-start.27
  4.8 2.0 copy-start.29
  4.8 2.1 copy-start.30
  6.9 1.4 copy-start.5
  8.3 1.0 copy-start.7
  9.3 1.0 copy-start.8
  103.5 5.2 %copy-start.9 = (bf16[1024,128]{1,0:T(8,128)(2,1)}, bf16[1024,128]{1,0:T(8,128)(2,1)S(1)}, u32[]{:S(2)}) copy-start(bf16[1024,128]{1,0:T(8,128)(2,1)S(1)} %get-tuple-element.16) | copy-start | bytes 786436
  103.5 14.5 %copy-start.3 = (bf16[2048,352]{1,0:T(8,128)(2,1)}, bf16[2048,352]{1,0:T(8,128)(2,1)S(1)}, u32[]{:S(2)}) copy-start(bf16[2048,352]{1,0:T(8,128)(2,1)S(1)} %get-tuple-element.20) | copy-start | bytes 4325380
  103.5 18.3 %copy-start.1 = (bf16[2048,352]{1,0:T(8,128)(2,1)}, bf16[2048,352]{1,0:T(8,128)(2,1)S(1)}, u32[]{:S(2)}) copy-start(bf16[2048,352]{1,0:T(8,128)(2,1)S(1)} %get-tuple-element.18) | copy-start | bytes 4325380
  103.6 5.1 %copy-start.19 = (bf16[1,1024,64]{2,1,0:T(8,128)(2,1)S(1)}, bf16[1,1024,64]{2,1,0:T(8,128)(2,1)}, u32[]{:S(2)}) copy-start(bf16[1,1024,64]{2,1,0:T(8,128)(2,1)} %copy-done.18) | copy-start | bytes 393220
  103.6 5.1 %copy-start.22 = (bf16[1,1024,64]{2,1,0:T(8,128)(2,1)S(1)}, bf16[1,1024,64]{2,1,0:T(8,128)(2,1)}, u32[]{:S(2)}) copy-start(bf16[1,1024,64]{2,1,0:T(8,128)(2,1)} %copy-done.21) | copy-start | bytes 393220
  108.7 1.4 copy-start.14
  111.8 1.4 copy-start.6
  113.1 1.8 copy-start.16
  114.9 1.7 copy-start.28
  124.6 0.9 copy-start.11
  126.3 2.2 copy-start.24
  128.5 1.7 copy-start.15
  130.2 2.1 copy-start.4
  130.2 2.1 copy-start.12
  132.3 5.1 %copy-start.2 = (bf16[2048,352]{1,0:T(8,128)(2,1)S(1)}, bf16[2048,352]{1,0:T(8,128)(2,1)}, u32[]{:S(2)}) copy-start(bf16[2048,352]{1,0:T(8,128)(2,1)} %copy-done.1) | copy-start | bytes 4325380
  137.4 5.1 %copy-start.17 = (bf16[1,2048,352]{1,2,0:T(8,128)(2,1)S(1)}, bf16[1,2048,352]{1,2,0:T(8,128)(2,1)}, u32[]{:S(2)}) copy-start(bf16[1,2048,352]{1,2,0:T(8,128)(2,1)} %param.16) | copy-start | bytes 4325380
  142.5 5.1 %copy-start.10 = (bf16[1024,128]{1,0:T(8,128)(2,1)S(1)}, bf16[1024,128]{1,0:T(8,128)(2,1)}, u32[]{:S(2)}) copy-start(bf16[1024,128]{1,0:T(8,128)(2,1)} %copy-done.9) | copy-start | bytes 786436
  142.5 5.1 %copy-start.20 = (bf16[1,1024,64]{2,1,0:T(8,128)(2,1)S(1)}, bf16[1,1024,64]{2,1,0:T(8,128)(2,1)}, u32[]{:S(2)}) copy-start(bf16[1,1024,64]{2,1,0:T(8,128)(2,1)} %copy-done.18) | copy-start | bytes 393220
  142.5 5.1 %copy-start.23 = (bf16[1,1024,64]{2,1,0:T(8,128)(2,1)S(1)}, bf16[1,1024,64]{2,1,0:T(8,128)(2,1)}, u32[]{:S(2)}) copy-start(bf16[1,1024,64]{2,1,0:T(8,128)(2,1)} %copy-done.21) | copy-start | bytes 393220
  142.5 5.1 %copy-start.25 = (bf16[896,128]{0,1:T(8,128)(2,1)S(1)}, bf16[896,128]{0,1:T(8,128)(2,1)}, u32[]{:S(2)}) copy-start(bf16[896,128]{0,1:T(8,128)(2,1)} %copy-done.24) | copy-start | bytes 688132
  161.3 2.0 copy-start

commit v3 on v1

v3 whole, which is shorter than its diff:
```python
import functools

import jax
import jax.numpy as jnp
from jax import lax
from jax.experimental import pallas as pl
from jax.experimental.pallas import tpu as pltpu
from jax.sharding import PartitionSpec as P

PLANE = 4
ANY = pl.BlockSpec(memory_space=pl.ANY)
VMEM = pl.BlockSpec(memory_space=pltpu.VMEM)


def trans_right(left, right):
    return lax.dot_general(
        left, right, (((1,), (1,)), ((), ())), preferred_element_type=jnp.float32
    )


def trans_left(left, right):
    return lax.dot_general(
        left, right, (((0,), (0,)), ((), ())), preferred_element_type=jnp.float32
    )


def position(planes):
    me = lax.axis_index("expert")
    half = lax.rem(me, 2)
    chip = lax.div(me, 2)
    return lax.div(chip, PLANE), lax.rem(chip, PLANE), half


def device(z, q, half):
    return {"expert": (z * PLANE + q) * 2 + half}


def remote(src, dst, send, recv, target):
    return pltpu.make_async_remote_copy(
        src_ref=src,
        dst_ref=dst,
        send_sem=send,
        recv_sem=recv,
        device_id=target,
        device_id_type=pl.DeviceIdType.MESH,
    )


def greet(target):
    pl.semaphore_signal(
        pltpu.get_barrier_semaphore(),
        inc=1,
        device_id=target,
        device_id_type=pl.DeviceIdType.MESH,
    )


def layer_kernel(
    planes,
    experts,
    cap,
    x_ref,
    c_ref,
    meta_ref,
    wg_ref,
    wu_ref,
    wd_ref,
    ag_ref,
    au_ref,
    bt_ref,
    out_ref,
    sum_ag,
    sum_au,
    sum_b,
    zbuf,
    zmeta,
    stage,
    rows,
    pickers,
    wg,
    wu,
    wd,
    at,
    bt,
    xs,
    ds,
    gg,
    gu,
    acc_a,
    acc_b,
    got_a,
    got_b,
    y,
    ybuf,
    zstage,
    zin,
    load_sem,
    w_load,
    w_send,
    w_recv,
    up_send,
    down_send,
    z_recv,
    um_send,
    dm_send,
    m_recv,
    p_send,
    p_recv,
    own_sem,
    y_send,
    y_recv,
    y_own,
    s_send,
    s_recv,
    g_send,
    g_recv,
):
    z, q, half = position(planes)
    tok, width = x_ref.shape
    wide = width // 2
    hidden_half = wg_ref.shape[0]
    hidden = 2 * hidden_half
    rank = ag_ref.shape[0]
    count = PLANE * cap
    last = planes - 1
    partner = device(z, q, 1 - half)

    own_x = pltpu.make_async_copy(x_ref, zbuf.at[z, pl.ds(0, tok)], load_sem.at[0])
    own_c = pltpu.make_async_copy(c_ref, zbuf.at[z, pl.ds(tok, tok)], load_sem.at[1])
    own_x.start()
    own_c.start()
    zmeta[z] = meta_ref[...]

    mine = pl.ds(pl.multiple_of(half * hidden_half, hidden_half), hidden_half)
    pieces = (
        (bt_ref, bt.at[mine]),
        (ag_ref, at.at[half, pl.ds(0, rank)]),
        (au_ref, at.at[half, pl.ds(rank, rank)]),
        (wg_ref, wg.at[mine]),
        (wu_ref, wu.at[mine]),
        (wd_ref, wd.at[mine]),
    )

    def piece_local(i):
        return pltpu.make_async_copy(pieces[i][0], pieces[i][1], w_load.at[i])

    def piece(i):
        return remote(pieces[i][0], pieces[i][1], w_send.at[i], w_recv.at[i], partner)

    for i in range(len(pieces)):
        piece_local(i).start()

    greet(partner)

    def hello_plane(step, carry):
        greet(device(z, lax.rem(q + step, PLANE), half))
        return carry

    def hello_column(step, carry):
        greet(device(lax.rem(z + step, planes), q, half))
        return carry

    lax.fori_loop(1, PLANE, hello_plane, 0)
    lax.fori_loop(1, planes, hello_column, 0)
    pl.semaphore_wait(pltpu.get_barrier_semaphore(), PLANE + planes - 1)
    own_x.wait()
    own_c.wait()

    def up(b):
        target = device(z + 1, q, half)
        return (
            remote(zmeta.at[b], zmeta.at[b], um_send.at[b], m_recv.at[b], target),
            remote(zbuf.at[b], zbuf.at[b], up_send.at[b], z_recv.at[b], target),
        )

    def down(b):
        target = device(z - 1, q, half)
        return (
            remote(zmeta.at[b], zmeta.at[b], dm_send.at[b], m_recv.at[b], target),
            remote(zbuf.at[b], zbuf.at[b], down_send.at[b], z_recv.at[b], target),
        )

    def begin(copies):
        for copy in copies:
            copy.start()

    def arrived(copies):
        for copy in copies:
            copy.wait_recv()

    def sent(copies):
        for copy in copies:
            copy.wait_send()

    def part(b, to):
        return remote(
            stage.at[b, to],
            rows.at[b, q],
            p_send.at[b, to],
            p_recv.at[b, q],
            device(z, to, half),
        )

    def part_came(b, source):
        return remote(
            stage.at[b, source],
            rows.at[b, source],
            p_send.at[b, source],
            p_recv.at[b, source],
            device(z, source, half),
        )

    def part_local(b):
        return pltpu.make_async_copy(stage.at[b, q], rows.at[b, q], own_sem.at[b])

    def give(b, to):
        return remote(
            y.at[b, to],
            ybuf.at[b, q],
            y_send.at[b, to],
            y_recv.at[b, q],
            device(z, to, half),
        )

    def give_came(b, source):
        return remote(
            y.at[b, source],
            ybuf.at[b, source],
            y_send.at[b, source],
            y_recv.at[b, source],
            device(z, source, half),
        )

    def give_local(b):
        return pltpu.make_async_copy(y.at[b, q], ybuf.at[b, q], y_own.at[b])

    def home(to):
        return remote(
            zstage.at[to], zin.at[z], s_send.at[to], s_recv.at[z], device(to, q, half)
        )

    def home_came(source):
        return remote(
            zstage.at[source],
            zin.at[source],
            s_send.at[source],
            s_recv.at[source],
            device(source, q, half),
        )

    def block_at(i):
        near = 2 * jnp.minimum(z, last - z)
        odd = lax.rem(i, 2)
        step = lax.div(i + odd, 2)
        around = jnp.where(odd == 1, z - step, z + step)
        onward = jnp.where(2 * z <= last, i, last - i)
        return jnp.where(i <= near, around, onward)

    def picked(b, to):
        expert = z * PLANE + to
        slots = zmeta[b, pl.ds(expert, 1), :]
        weights = zmeta[b, pl.ds(experts + expert, 1), :]
        numbers = lax.broadcasted_iota(jnp.int32, (cap, tok), 0).astype(jnp.float32)
        mask = numbers == slots
        ones = jnp.where(mask, 1.0, 0.0)
        zeros = jnp.zeros_like(ones)
        scale = jnp.sum(jnp.where(mask, weights, 0.0), axis=1, keepdims=True)
        scale = jnp.concatenate([jnp.ones_like(scale), scale], axis=0)
        picker = jnp.concatenate(
            [
                jnp.concatenate([ones, zeros], axis=1),
                jnp.concatenate([zeros, ones], axis=1),
            ],
            axis=0,
        ).astype(jnp.bfloat16)
        pickers[b, to] = picker
        tile = width // 4
        for n in range(4):
            cols = pl.ds(n * tile, tile)
            found = jnp.dot(picker, zbuf[b, :, cols], preferred_element_type=jnp.float32)
            stage[b, to, :, cols] = (found * scale).astype(jnp.bfloat16)

    def spread(i):
        b = block_at(i)

        @pl.when(b < z)
        def _():
            arrived(down(b))

            @pl.when(z < last)
            def _():
                begin(up(b))

        @pl.when(b > z)
        def _():
            arrived(up(b))

            @pl.when(z > 0)
            def _():
                begin(down(b))

        def one(step, carry):
            to = lax.rem(q + step, PLANE)
            picked(b, to)
            part(b, to).start()
            return carry

        lax.fori_loop(1, PLANE, one, 0)
        picked(b, q)
        part_local(b).start()

    def expert(i):
        b = block_at(i)

        def one(step, carry):
            part_came(b, lax.rem(q + step, PLANE)).wait_recv()
            return carry

        lax.fori_loop(1, PLANE, one, 0)
        part_local(b).wait()
        f32, bf16 = jnp.float32, jnp.bfloat16
        for n in range(4):
            cols = pl.ds(n * (width // 4), width // 4)
            both = [rows[b, source, :, cols].astype(f32) for source in range(PLANE)]
            xs[:, cols] = jnp.concatenate([v[:cap] for v in both], axis=0).astype(bf16)
            ds[:, cols] = jnp.concatenate([v[cap:] for v in both], axis=0).astype(bf16)
        low = (
            trans_right(xs[:, :wide], at[0]) + trans_right(xs[:, wide:], at[1])
        ).astype(bf16)
        lanes = lax.broadcasted_iota(jnp.int32, (count, 2 * rank), 1)
        low_gate = jnp.where(lanes < rank, low, jnp.zeros_like(low))
        low_up = jnp.where(lanes < rank, jnp.zeros_like(low), low)
        for lo in range(0, hidden, 256):
            hi = min(lo + 256, hidden)
            gate = trans_right(xs[...], wg[lo:hi]) + trans_right(low_gate, bt[lo:hi])
            upward = trans_right(xs[...], wu[lo:hi]) + trans_right(low_up, bt[lo:hi])
            hidden_grad = trans_right(ds[...], wd[lo:hi])
            sig = 1.0 / (1.0 + jnp.exp(-gate))
            gg[:, lo:hi] = (hidden_grad * upward * sig * (1.0 + gate * (1.0 - sig))).astype(bf16)
            gu[:, lo:hi] = (hidden_grad * gate * sig).astype(bf16)
        back = jnp.where(
            lanes < rank,
            jnp.dot(gg[...], bt[...], preferred_element_type=f32),
            jnp.dot(gu[...], bt[...], preferred_element_type=f32),
        ).astype(bf16)
        tile = wide // 4

        def columns(t, carry):
            sides = []
            for side in range(2):
                cols = pl.ds(pl.multiple_of(side * wide + t * tile, tile), tile)
                inner = pl.ds(pl.multiple_of(t * tile, tile), tile)
                sides.append(
                    jnp.dot(gg[...], wg[:, cols], preferred_element_type=f32)
                    + jnp.dot(gu[...], wu[:, cols], preferred_element_type=f32)
                    + jnp.dot(back, at[side, :, inner], preferred_element_type=f32)
                )
            for source in range(PLANE):
                these = slice(source * cap, (source + 1) * cap)
                y[b, source, :, inner] = jnp.concatenate(
                    [side[these] for side in sides], axis=0
                ).astype(bf16)
            return carry

        lax.fori_loop(0, 4, columns, 0)

        def send(step, carry):
            give(b, lax.rem(q + step, PLANE)).start()
            return carry

        lax.fori_loop(1, PLANE, send, 0)
        give_local(b).start()
        for n in range(4):
            cols = pl.ds(n * (width // 4), width // 4)
            acc_a[:, cols] += trans_left(back, xs[:, cols])
        of_b = lax.broadcasted_iota(jnp.int32, (hidden, 2 * rank), 1)
        acc_b[...] += jnp.where(of_b < rank, trans_left(gg[...], low), trans_left(gu[...], low))

    def collect(i):
        b = block_at(i)

        def one(step, carry):
            give_came(b, lax.rem(q + step, PLANE)).wait_recv()
            return carry

        lax.fori_loop(1, PLANE, one, 0)
        give_local(b).wait()
        picker = pickers[b].reshape(PLANE * 2 * cap, 2 * tok)
        tile = wide // 2
        for n in range(2):
            cols = pl.ds(n * tile, tile)
            held = ybuf[b, :, :, cols].reshape(PLANE * 2 * cap, tile)
            zstage[b, :, cols] = trans_left(picker, held).astype(jnp.bfloat16)

        @pl.when(b != z)
        def _():
            home(b).start()

    @pl.when(z < last)
    def _():
        begin(up(z))

    @pl.when(z > 0)
    def _():
        begin(down(z))

    for i in range(len(pieces)):
        piece(i).start()
    acc_a[...] = jnp.zeros_like(acc_a)
    acc_b[...] = jnp.zeros_like(acc_b)

    def step(i, carry):
        @pl.when(i < planes)
        def _():
            spread(i)

        @pl.when(i == 1)
        def _():
            for n in range(len(pieces)):
                piece_local(n).wait()
                piece(n).wait()

        @pl.when((i >= 1) & (i <= planes))
        def _():
            expert(i - 1)

        @pl.when(i >= 2)
        def _():
            collect(i - 2)

        return carry

    lax.fori_loop(0, planes + 2, step, 0)

    theirs = pl.ds(pl.multiple_of((1 - half) * hidden_half, hidden_half), hidden_half)
    other_cols = pl.ds(pl.multiple_of((1 - half) * wide, wide), wide)
    own_cols = pl.ds(pl.multiple_of(half * wide, wide), wide)
    grads = (
        remote(acc_a.at[:, other_cols], got_a, g_send.at[0], g_recv.at[0], partner),
        remote(acc_b.at[theirs], got_b, g_send.at[1], g_recv.at[1], partner),
    )
    for copy in grads:
        copy.start()
    for copy in grads:
        copy.wait()
    total_a = acc_a[:, own_cols] + got_a[...]
    sum_ag[...] = total_a[:rank]
    sum_au[...] = total_a[rank:]
    sum_b[...] = acc_b[mine] + got_b[...]

    def add(step, total):
        source = lax.rem(z + step, planes)
        home_came(source).wait_recv()
        return total + zin[source].astype(jnp.float32)

    total = lax.fori_loop(1, planes, add, zstage[z].astype(jnp.float32))
    out_ref[:, :wide] = total[:tok].astype(jnp.bfloat16)
    out_ref[:, wide:] = total[tok:].astype(jnp.bfloat16)

    def finish(b, carry):
        def one(step, inner):
            to = lax.rem(q + step, PLANE)
            part(b, to).wait_send()
            give(b, to).wait_send()
            return inner

        lax.fori_loop(1, PLANE, one, 0)

        @pl.when((b <= z) & (z < last))
        def _():
            sent(up(b))

        @pl.when((b >= z) & (z > 0))
        def _():
            sent(down(b))

        @pl.when(b != z)
        def _():
            home(b).wait_send()

        return carry

    lax.fori_loop(0, planes, finish, 0)


def layer(planes, experts, cap, tokens, cotangent, meta, pieces):
    tok, width = tokens.shape
    hidden_half = pieces[0].shape[0]
    rank = pieces[3].shape[0]
    hidden, wide, count = 2 * hidden_half, width // 2, PLANE * cap
    bf16, f32 = jnp.bfloat16, jnp.float32
    dma = pltpu.SemaphoreType.DMA
    shape = jax.ShapeDtypeStruct
    per_block, per_pair, six = dma((planes,)), dma((planes, PLANE)), dma((len(pieces),))
    return pl.pallas_call(
        functools.partial(layer_kernel, planes, experts, cap),
        out_shape=[
            shape((tok, width), bf16),
            shape((rank, wide), f32),
            shape((rank, wide), f32),
            shape((hidden_half, 2 * rank), f32),
        ],
        in_specs=[ANY, ANY, VMEM] + [ANY] * len(pieces),
        out_specs=[VMEM] * 4,
        scratch_shapes=[
            pltpu.VMEM((planes, 2 * tok, width), bf16),
            pltpu.VMEM((planes,) + meta.shape, f32),
            pltpu.VMEM((planes, PLANE, 2 * cap, width), bf16),
            pltpu.VMEM((planes, PLANE, 2 * cap, width), bf16),
            pltpu.VMEM((planes, PLANE, 2 * cap, 2 * tok), bf16),
            pltpu.VMEM((hidden, width), bf16),
            pltpu.VMEM((hidden, width), bf16),
            pltpu.VMEM((hidden, width), bf16),
            pltpu.VMEM((2, 2 * rank, wide), bf16),
            pltpu.VMEM((hidden, 2 * rank), bf16),
            pltpu.VMEM((count, width), bf16),
            pltpu.VMEM((count, width), bf16),
            pltpu.VMEM((count, hidden), bf16),
            pltpu.VMEM((count, hidden), bf16),
            pltpu.VMEM((2 * rank, width), f32),
            pltpu.VMEM((hidden, 2 * rank), f32),
            pltpu.VMEM((2 * rank, wide), f32),
            pltpu.VMEM((hidden_half, 2 * rank), f32),
            pltpu.VMEM((planes, PLANE, 2 * cap, wide), bf16),
            pltpu.VMEM((planes, PLANE, 2 * cap, wide), bf16),
            pltpu.VMEM((planes, 2 * tok, wide), bf16),
            pltpu.VMEM((planes, 2 * tok, wide), bf16),
            dma((2,)),
            six,
            six,
            six,
        ]
        + [per_block] * 6
        + [per_pair, per_pair, per_block]
        + [per_pair, per_pair, per_block]
        + [per_block, per_block, dma((2,)), dma((2,))],
        compiler_params=pltpu.CompilerParams(
            collective_id=0, has_side_effects=True, vmem_limit_bytes=62 * 2**20
        ),
        name="layer",
    )(tokens, cotangent, meta, *pieces)


def on_device(
    tokens,
    cotangent,
    token_experts,
    routing_weight_cache,
    gate_weight,
    up_weight,
    down_weight,
    gate_adapter_input,
    gate_adapter_output,
    up_adapter_input,
    up_adapter_output,
):
    n_devices = lax.axis_size("expert")
    n_experts = n_devices // 2
    planes = n_experts // PLANE
    tok, width = tokens.shape
    top = token_experts.shape[1]
    slot_cap = 2 * max(2, 9 * tok * top // (16 * n_experts) + 1)
    slot_cap = (slot_cap + 7) // 8 * 8
    rank = gate_adapter_input.shape[2]

    named = token_experts[None, :, :] == jnp.arange(n_experts, dtype=jnp.int32)[:, None, None]
    chosen = jnp.any(named, axis=2).astype(jnp.float32)
    earlier = (
        lax.broadcasted_iota(jnp.int32, (tok, tok), 0)
        < lax.broadcasted_iota(jnp.int32, (tok, tok), 1)
    ).astype(jnp.float32)
    slots = jnp.dot(chosen, earlier, preferred_element_type=jnp.float32)
    slots = jnp.where(chosen > 0, slots, -1.0)
    weights = jnp.sum(jnp.where(named, routing_weight_cache[None, :, :], 0.0), axis=2)
    meta = jnp.concatenate([slots, weights], axis=0)

    pieces = (
        gate_weight[0].T,
        up_weight[0].T,
        down_weight[0],
        gate_adapter_input[0].T,
        up_adapter_input[0].T,
        jnp.concatenate([gate_adapter_output[0], up_adapter_output[0]], axis=0).T,
    )
    grad_tokens, sum_ag, sum_au, sum_b = layer(
        planes, n_experts, slot_cap, tokens, cotangent, meta, pieces
    )
    return (
        grad_tokens,
        sum_ag.T[None],
        sum_b[:, :rank].T[None],
        sum_au.T[None],
        sum_b[:, rank:].T[None],
    )


def solution(mesh):
    in_specs = (
        P(("groups", "expert"), None),
        P(("groups", "expert"), None),
        P(("groups", "expert"), None),
        P(("groups", "expert"), None),
        P("expert", None, None),
        P("expert", None, None),
        P("expert", None, None),
        P("expert", None, None),
        P("expert", None, None),
        P("expert", None, None),
        P("expert", None, None),
    )
    out_specs = (
        P(("groups", "expert"), None),
        P(("groups", "expert"), None, None),
        P(("groups", "expert"), None, None),
        P(("groups", "expert"), None, None),
        P(("groups", "expert"), None, None),
    )
    return jax.shard_map(
        on_device, mesh=mesh, in_specs=in_specs, out_specs=out_specs, check_vma=False
    )
```

time: 299 us -> 178 us (0.60); the launches traced: 294 us -> 178 us
  waiting for transfers between devices: 200 us -> 0 us
  Pallas kernels: 0 us -> 167 us
  matrix products: 51.4 us -> 0.14 us
  starting transfers between devices: 28 us -> 0 us
  other arithmetic: 11 us -> 2.77 us
  local copies, waits for them, and re-layouts: 3.3 us -> 6.76 us
    all_to_all x3 -> x0, waiting for transfers between devices: 195 us -> none  [exchanged(): lax.all_to_all(rows.reshape(n_experts, slot_cap, width), 'expert', split_...]
    pallas_call x0 -> x1, Pallas kernels: none -> 167 us  [layer(): pl.pallas_call(functools.partial(layer_kernel, planes, experts, cap), out...]
    dot_general x17 -> x1, matrix products: 51.4 us -> 0.14 us  [on_device(): slots = jnp.dot(chosen, earlier, preferred_element_type=jnp.float32)]
    all_to_all x3 -> x0, starting transfers between devices: 26 us -> none  [exchanged(): lax.all_to_all(rows.reshape(n_experts, slot_cap, width), 'expert', split_...]
    select_n x6 -> x0, other arithmetic: 7.35 us -> none  [joined(): first = jnp.where(my_half == 0, own, other)]
    ppermute x8 -> x0, waiting for transfers between devices: 4.88 us -> none  [swapped(): return lax.ppermute(value, axis, pairs)]
    unnamed x51 -> x13, local copies, waits for them, and re-layouts: 1.04 us -> 5.56 us
  transfers between devices with their start and end apart: 11 -> 0, of which waited for: 6 -> 0; matrix products, arithmetic and copies ran while one was open for 10% -> 0% of each run, Pallas kernels for 0% -> 0%
where the time goes in v3:
time: 178 us
  Pallas kernels  167 us (94%)
  local copies, waits for them, and re-layouts  6.76 us (4%)
  other arithmetic  2.77 us (2%)
    pallas_call x1, Pallas kernels, layer(): pl.pallas_call(functools.partial(layer_kernel, planes, experts, cap), out...  167 us
    unnamed x13, local copies, waits for them, and re-layouts  5.56 us

profile of v3, /device:TPU:24, one launch (start us, length us, event | category | flops | bytes accessed | tf_op | source)
XLA Modules:
  0.0 177.8 jit_solution(7171170602270427082)
XLA Ops:
  0.6 0.7 fusion
  1.3 0.1 convolution_select_fusion
  1.5 0.7 select_reduce_fusion
  2.2 0.6 pad_maximum_fusion.meta_ref
  2.8 0.9 copy.22
  3.7 0.9 copy.23
  4.6 0.7 maximum_bitcast_fusion.bt_ref
  5.4 167.4 %layer.1 = (bf16[128,2048]{1,0:T(8,128)(2,1)}, f32[64,1024]{1,0:T(8,128)}, f32[64,1024]{1,0:T(8,128)}, f32[352,128]{1,0:T(8,128)}) custom-call(bf16[128,2048]{1,0:T(8,128)(2,1)} %x_ref.1, bf16[128,2048]{1,0:T(8,128)(2,1)} %c_ref.1, f32[32,128]{1,0:T(8,128)} %pad_maximum_fusion.meta_ref, bf16[352,2048]{1,0:T(8,128)(2,1)} %bitcast.32, ...), custom_call_target="tpu_custom_call" | custom-call | tf_op jit(solution)/shard_map/layer/pallas_call | solution.py:495
  172.8 0.0 copy-start
  172.8 0.0 copy-start.2
  172.8 0.0 copy-start.1
  172.8 1.2 slice_bitcast_fusion
  174.0 0.8 copy.25
  174.8 0.8 copy.24
  175.6 0.0 copy-done
  175.6 0.8 copy.29
  176.4 0.0 copy-done.2
  176.4 0.7 copy.30
  177.1 0.0 copy-done.1
  177.1 0.7 copy.31
Async XLA Ops:
  172.8 2.8 %copy-start = (bf16[128,2048]{1,0:T(8,128)(2,1)S(1)}, bf16[128,2048]{1,0:T(8,128)(2,1)}, u32[]{:S(2)}) copy-start(bf16[128,2048]{1,0:T(8,128)(2,1)} %get-tuple-element.30) | copy-start | bytes 1572868
  172.8 3.5 %copy-start.2 = (f32[64,1024]{1,0:T(8,128)S(1)}, f32[64,1024]{1,0:T(8,128)}, u32[]{:S(2)}) copy-start(f32[64,1024]{1,0:T(8,128)} %get-tuple-element.10) | copy-start | bytes 786436
  172.8 4.2 %copy-start.1 = (f32[64,1024]{1,0:T(8,128)S(1)}, f32[64,1024]{1,0:T(8,128)}, u32[]{:S(2)}) copy-start(f32[64,1024]{1,0:T(8,128)} %get-tuple-element.12) | copy-start | bytes 786436

commit v4 on v3

--- a/solution.py
+++ b/solution.py
@@ -71,7 +71,8 @@
     out_ref,
     sum_ag,
     sum_au,
-    sum_b,
+    sum_bg,
+    sum_bu,
     zbuf,
     zmeta,
     stage,
@@ -252,8 +253,9 @@
         near = 2 * jnp.minimum(z, last - z)
         odd = lax.rem(i, 2)
         step = lax.div(i + odd, 2)
-        around = jnp.where(odd == 1, z - step, z + step)
-        onward = jnp.where(2 * z <= last, i, last - i)
+        low = 2 * z <= last
+        around = jnp.where((odd == 1) == low, z + step, z - step)
+        onward = jnp.where(low, i, last - i)
         return jnp.where(i <= near, around, onward)
 
     def picked(b, to):
@@ -280,24 +282,27 @@
             found = jnp.dot(picker, zbuf[b, :, cols], preferred_element_type=jnp.float32)
             stage[b, to, :, cols] = (found * scale).astype(jnp.bfloat16)
 
+    def forward(i):
+        below, above = z - i, z + i
+
+        @pl.when(below >= 0)
+        def _():
+            arrived(down(below))
+
+            @pl.when(z < last)
+            def _():
+                begin(up(below))
+
+        @pl.when(above <= last)
+        def _():
+            arrived(up(above))
+
+            @pl.when(z > 0)
+            def _():
+                begin(down(above))
+
     def spread(i):
         b = block_at(i)
-
-        @pl.when(b < z)
-        def _():
-            arrived(down(b))
-
-            @pl.when(z < last)
-            def _():
-                begin(up(b))
-
-        @pl.when(b > z)
-        def _():
-            arrived(up(b))
-
-            @pl.when(z > 0)
-            def _():
-                begin(down(b))
 
         def one(step, carry):
             to = lax.rem(q + step, PLANE)
@@ -308,6 +313,14 @@
         lax.fori_loop(1, PLANE, one, 0)
         picked(b, q)
         part_local(b).start()
+
+    def answer(b):
+        def send(step, carry):
+            give(b, lax.rem(q + step, PLANE)).start()
+            return carry
+
+        lax.fori_loop(1, PLANE, send, 0)
+        give_local(b).start()
 
     def expert(i):
         b = block_at(i)
@@ -364,12 +377,10 @@
 
         lax.fori_loop(0, 4, columns, 0)
 
-        def send(step, carry):
-            give(b, lax.rem(q + step, PLANE)).start()
-            return carry
-
-        lax.fori_loop(1, PLANE, send, 0)
-        give_local(b).start()
+        @pl.when(i > 0)
+        def _():
+            answer(b)
+
         for n in range(4):
             cols = pl.ds(n * (width // 4), width // 4)
             acc_a[:, cols] += trans_left(back, xs[:, cols])
@@ -410,6 +421,10 @@
     acc_b[...] = jnp.zeros_like(acc_b)
 
     def step(i, carry):
+        @pl.when((i >= 1) & (i < planes))
+        def _():
+            forward(i)
+
         @pl.when(i < planes)
         def _():
             spread(i)
@@ -424,13 +439,18 @@
         def _():
             expert(i - 1)
 
-        @pl.when(i >= 2)
+        @pl.when(i == planes)
+        def _():
+            answer(z)
+
+        @pl.when(i >= 3)
         def _():
             collect(i - 2)
 
         return carry
 
     lax.fori_loop(0, planes + 2, step, 0)
+    collect(0)
 
     theirs = pl.ds(pl.multiple_of((1 - half) * hidden_half, hidden_half), hidden_half)
     other_cols = pl.ds(pl.multiple_of((1 - half) * wide, wide), wide)
@@ -446,7 +466,9 @@
     total_a = acc_a[:, own_cols] + got_a[...]
     sum_ag[...] = total_a[:rank]
     sum_au[...] = total_a[rank:]
-    sum_b[...] = acc_b[mine] + got_b[...]
+    total_b = (acc_b[mine] + got_b[...]).T
+    sum_bg[...] = total_b[:rank]
+    sum_bu[...] = total_b[rank:]
 
     def add(step, total):
         source = lax.rem(z + step, planes)
@@ -498,10 +520,11 @@
             shape((tok, width), bf16),
             shape((rank, wide), f32),
             shape((rank, wide), f32),
-            shape((hidden_half, 2 * rank), f32),
+            shape((rank, hidden_half), f32),
+            shape((rank, hidden_half), f32),
         ],
         in_specs=[ANY, ANY, VMEM] + [ANY] * len(pieces),
-        out_specs=[VMEM] * 4,
+        out_specs=[VMEM] * 5,
         scratch_shapes=[
             pltpu.VMEM((planes, 2 * tok, width), bf16),
             pltpu.VMEM((planes,) + meta.shape, f32),
@@ -582,15 +605,15 @@
         up_adapter_input[0].T,
         jnp.concatenate([gate_adapter_output[0], up_adapter_output[0]], axis=0).T,
     )
-    grad_tokens, sum_ag, sum_au, sum_b = layer(
+    grad_tokens, sum_ag, sum_au, sum_bg, sum_bu = layer(
         planes, n_experts, slot_cap, tokens, cotangent, meta, pieces
     )
     return (
         grad_tokens,
         sum_ag.T[None],
-        sum_b[:, :rank].T[None],
+        sum_bg[None],
         sum_au.T[None],
-        sum_b[:, rank:].T[None],
+        sum_bu[None],
     )
 
 

time: 178 us -> 166 us (0.933)
  the two profiles are of different devices: /device:TPU:24 before, /device:TPU:0 now
where the time goes in v4:
time: 166 us; the launch traced here: 165 us
  Pallas kernels  154 us (93%)
  local copies, waits for them, and re-layouts  7.43 us (4%)
  other arithmetic  2.77 us (2%)
    pallas_call x1, Pallas kernels, layer(): pl.pallas_call(functools.partial(layer_kernel, planes, experts, cap), out...  154 us
    unnamed x13, local copies, waits for them, and re-layouts  7.43 us

profile of v4, /device:TPU:0, one launch (start us, length us, event | category | flops | bytes accessed | tf_op | source)
XLA Modules:
  0.0 165.4 jit_solution(1556985896045664213)
XLA Ops:
  0.6 0.7 fusion
  1.3 0.1 convolution_select_fusion
  1.5 0.7 select_reduce_fusion
  2.2 0.6 pad_maximum_fusion.meta_ref
  2.8 0.9 copy.20
  3.7 0.9 copy.21
  4.6 0.7 maximum_bitcast_fusion.bt_ref
  5.4 154.4 %layer.1 = (bf16[128,2048]{1,0:T(8,128)(2,1)}, f32[64,1024]{1,0:T(8,128)}, f32[64,1024]{1,0:T(8,128)}, f32[64,352]{1,0:T(8,128)}, f32[64,352]{1,0:T(8,128)}) custom-call(bf16[128,2048]{1,0:T(8,128)(2,1)} %x_ref.1, bf16[128,2048]{1,0:T(8,128)(2,1)} %c_ref.1, f32[32,128]{1,0:T(8,128)} %pad_maximum_fusion.meta_ref, bf16[352,2048]{1,0:T(8,128)(2,1)} %bitcast.26, ...), custom_call_target="tpu_custom_call" | custom-call | tf_op jit(solution)/shard_map/layer/pallas_call | solution.py:517
  159.8 0.0 copy-start.2
  159.8 0.0 copy-start
  159.8 0.0 copy-start.1
  159.8 1.9 %copy.27 = bf16[128,2048]{1,0:T(8,128)(2,1)} copy(bf16[128,2048]{1,0:T(8,128)(2,1)} %get-tuple-element.20) | data formatting | bytes 1048576
  161.8 1.7 %copy.28 = f32[1,1024,64]{1,2,0:T(8,128)} copy(f32[1,1024,64]{1,2,0:T(8,128)} %bitcast.32) | data formatting | bytes 524288
  163.4 0.0 copy-done.2
  163.4 0.6 copy.29
  164.1 0.0 copy-done
  164.1 0.7 copy.30
  164.8 0.0 copy-done.1
  164.8 0.6 copy.31
Async XLA Ops:
  159.8 3.6 %copy-start.2 = (f32[64,352]{1,0:T(8,128)S(1)}, f32[64,352]{1,0:T(8,128)}, u32[]{:S(2)}) copy-start(f32[64,352]{1,0:T(8,128)} %get-tuple-element.12) | copy-start | bytes 270340
  159.8 4.3 %copy-start = (f32[64,1024]{1,0:T(8,128)S(1)}, f32[64,1024]{1,0:T(8,128)}, u32[]{:S(2)}) copy-start(f32[64,1024]{1,0:T(8,128)} %get-tuple-element.13) | copy-start | bytes 786436
  159.8 5.0 %copy-start.1 = (f32[64,352]{1,0:T(8,128)S(1)}, f32[64,352]{1,0:T(8,128)}, u32[]{:S(2)}) copy-start(f32[64,352]{1,0:T(8,128)} %get-tuple-element.14) | copy-start | bytes 270340
